TPU v7x, 512 devices: a whole 4x4x16 slice. The times are simulated.
512 devices in a mesh: dom: 128 (over z, y, core), feat: 4 (over x).
Axes of the slice: x: 4, y: 4, z: 16, core: 2. Of those that a mesh axis runs over, the one named last changes fastest.
Arguments:
- features: bfloat16 [32768, 512], P('dom', 'feat'), may hold values from -6 to 6
- w_self: bfloat16 [512, 512], P('feat'), may hold values from -0.25 to 0.25
- w_neigh: bfloat16 [512, 512], P('feat'), may hold values from -0.25 to 0.25
- bias: bfloat16 [512], P('feat'), may hold values from -3 to 3
- cotangent: bfloat16 [32768, 512], P('dom', 'feat'), may hold values from -6 to 6
- tile_vals: bfloat16 [128, 4, 128, 128], P('dom'), may hold values from -0.375 to 0.375
- tile_pos: int32 [128, 4], P('dom'), may hold values from 0 to 3, as said below
- tile_count: int32 [128], P('dom'), may hold values from 1 to 4, as said below
- send_rows: int32 [128, 128, 3], P('dom'), may hold values from 0 to 255
- recv_dest: int32 [128, 128, 3], P('dom'), may hold values from 0 to 255
- ghost_weight: float32 [128, 128, 3], P('dom'), may hold values from 0.2 to 1.8
- recv_count: int32 [128, 128], P('dom'), may hold values from 0 to 3, as said below
- hub_rows: int32 [128, 2], P('dom'), may hold values from 0 to 255, as said below
- hub_weight: bfloat16 [32768, 256], P('dom'), may hold values from -0.375 to 0.375
Outputs:
- output: bfloat16 [32768, 512], P('dom', 'feat')
- grad_features: bfloat16 [32768, 512], P('dom', 'feat')
- grad_self: float32 [512, 512], P('feat')
- grad_neigh: float32 [512, 512], P('feat')
- grad_bias: float32 [512], P('feat')
Inputs may be any that keep to these rules, and one draw needn't show every extreme that they name: `tile_pos`: within a partition the numbers are distinct. `tile_count`: some partition uses all 4 slots. `recv_count`: some partition receives 3 live slots from some peer. `hub_rows`: within a partition the rows are distinct.
All inputs are finite; a program needn't handle non-finite values.
Results may differ from a plain program's by a relative error of at most 0.017.
Values may be sent and summed in bfloat16 or wider, within the bound.
A program may use at most 64 MiB of HBM per device.

v0:
```python
import math

import jax
import jax.numpy as jnp
from jax import lax
from jax.sharding import PartitionSpec as P


def tile_forward(tiles_here, places, count_here, blocks):
    block_count = blocks.shape[0]

    def add_tile(slot_index, totals):
        tile_place = places[slot_index]
        product = jnp.dot(
            tiles_here[slot_index],
            blocks[tile_place % block_count],
            preferred_element_type=jnp.float32,
        )
        return totals.at[tile_place // block_count].add(product)

    return lax.fori_loop(0, count_here, add_tile, jnp.zeros(blocks.shape, jnp.float32))


def tile_backward(tiles_here, places, count_here, blocks):
    block_count = blocks.shape[0]

    def add_tile(slot_index, totals):
        tile_place = places[slot_index]
        product = lax.dot_general(
            tiles_here[slot_index],
            blocks[tile_place // block_count],
            (((0,), (0,)), ((), ())),
            preferred_element_type=jnp.float32,
        )
        return totals.at[tile_place % block_count].add(product)

    return lax.fori_loop(0, count_here, add_tile, jnp.zeros(blocks.shape, jnp.float32))


def on_device(
    features,
    w_self,
    w_neigh,
    bias,
    cotangent,
    tile_vals,
    tile_pos,
    tile_count,
    send_rows,
    recv_dest,
    ghost_weight,
    recv_count,
    hub_rows,
    hub_weight,
):
    row_count, width_here = features.shape
    tile_size = tile_vals.shape[-1]
    block_count = row_count // tile_size
    slot_count = send_rows.shape[-1]
    hub_here = hub_rows.shape[-1]
    live = jnp.arange(slot_count, dtype=jnp.int32)[None, :] < recv_count[0][:, None]
    coef = jnp.where(live, ghost_weight[0], jnp.zeros_like(ghost_weight[0]))
    blocks = features.reshape(block_count, tile_size, width_here)
    local_part = tile_forward(tile_vals[0], tile_pos[0], tile_count[0], blocks).reshape(
        row_count, width_here
    )
    outgoing = features[send_rows[0]]
    incoming = lax.all_to_all(outgoing, "dom", split_axis=0, concat_axis=0, tiled=True)
    weighted = incoming.astype(jnp.float32) * coef[:, :, None]
    ghost_part = jax.ops.segment_sum(
        weighted.reshape(-1, width_here), recv_dest[0].reshape(-1), num_segments=row_count
    )
    owned_rows = features[hub_rows[0]]
    hub_part = jnp.dot(
        hub_weight,
        lax.all_gather(owned_rows, "dom", axis=0, tiled=True),
        preferred_element_type=jnp.float32,
    )
    neigh = (local_part + ghost_part + hub_part).astype(jnp.bfloat16)
    partial_sum = jnp.dot(features, w_self, preferred_element_type=jnp.float32) + jnp.dot(
        neigh, w_neigh, preferred_element_type=jnp.float32
    )
    preact = lax.psum_scatter(
        partial_sum.astype(jnp.bfloat16), "feat", scatter_dimension=1, tiled=True
    ).astype(jnp.float32)
    preact = preact + bias.astype(jnp.float32)
    output = jax.nn.silu(preact).astype(jnp.bfloat16)
    logistic = jax.nn.sigmoid(preact)
    grad_pre = (
        cotangent.astype(jnp.float32) * logistic * (1.0 + preact * (1.0 - logistic))
    ).astype(jnp.bfloat16)
    arrived_piece = lax.all_gather(grad_pre, "feat", axis=1, tiled=True)
    into_self = lax.dot_general(
        arrived_piece, w_self, (((1,), (1,)), ((), ())), preferred_element_type=jnp.float32
    )
    into_neigh = lax.dot_general(
        arrived_piece, w_neigh, (((1,), (1,)), ((), ())), preferred_element_type=jnp.float32
    )
    self_cols_grad = lax.dot_general(
        features, arrived_piece, (((0,), (0,)), ((), ())), preferred_element_type=jnp.float32
    )
    neigh_cols_grad = lax.dot_general(
        neigh, arrived_piece, (((0,), (0,)), ((), ())), preferred_element_type=jnp.float32
    )
    grad_self_part = self_cols_grad
    grad_neigh_part = neigh_cols_grad
    into_self, into_neigh, grad_self_part, grad_neigh_part = (
        into_self,
        into_neigh,
        grad_self_part,
        grad_neigh_part,
    )
    neigh_grad = into_neigh.astype(jnp.bfloat16)
    grad_blocks = neigh_grad.reshape(block_count, tile_size, width_here)
    local_back = tile_backward(tile_vals[0], tile_pos[0], tile_count[0], grad_blocks).reshape(
        row_count, width_here
    )
    returned = coef[:, :, None] * neigh_grad[recv_dest[0]].astype(jnp.float32)
    arrived_grads = lax.all_to_all(
        returned.astype(jnp.bfloat16), "dom", split_axis=0, concat_axis=0, tiled=True
    ).astype(returned.dtype)
    ghost_back = jax.ops.segment_sum(
        arrived_grads.reshape(-1, width_here), send_rows[0].reshape(-1), num_segments=row_count
    )
    hub_term = lax.dot_general(
        hub_weight, neigh_grad, (((0,), (0,)), ((), ())), preferred_element_type=jnp.float32
    )
    every_hub = lax.psum(hub_term, "dom")
    owned_grad = lax.dynamic_slice_in_dim(every_hub, lax.axis_index("dom") * hub_here, hub_here, 0)
    hub_back = jax.ops.segment_sum(owned_grad, hub_rows[0], num_segments=row_count)
    grad_features = (into_self + local_back + ghost_back + hub_back).astype(jnp.bfloat16)
    bias_part = jnp.sum(grad_pre.astype(jnp.float32), axis=0)
    total_self, total_neigh, total_bias = lax.psum(
        (grad_self_part, grad_neigh_part, bias_part), "dom"
    )
    scale = 1.0 / math.sqrt(lax.axis_size("dom") * row_count)
    return (output, grad_features, total_self * scale, total_neigh * scale, total_bias * scale)


def solution(mesh):
    placed = (
        P("dom", "feat"),
        P("feat", None),
        P("feat", None),
        P("feat"),
        P("dom", "feat"),
        P("dom", None, None, None),
        P("dom", None),
        P("dom"),
        P("dom", None, None),
        P("dom", None, None),
        P("dom", None, None),
        P("dom", None),
        P("dom", None),
        P("dom", None),
    )
    return jax.shard_map(
        on_device,
        mesh=mesh,
        in_specs=placed,
        out_specs=(P("dom", "feat"), P("dom", "feat"), P("feat", None), P("feat", None), P("feat")),
        check_vma=False,
    )
```

profile of v0, /device:TPU:1, one launch (start us, length us, event | category | flops | bytes accessed | tf_op | source)
XLA Modules:
  0.0 540.5 jit_solution(18394698778132560153)
XLA Ops:
  8.7 1.4 gather_fusion.1
  10.9 20.6 %all-to-all-start = ((bf16[128,3,128]{2,1,0:T(4,128)(2,1)}), bf16[128,3,128]{2,1,0:T(4,128)(2,1)S(1)}, u32[]{:S(2)}, u32[]{:S(2)}) async-start(bf16[128,3,128]{2,1,0:T(4,128)(2,1)} %reshape.243), calls=%async_computation | async-start | bytes 262144 | tf_op jit(solution)/shard_map/all_to_all | solution.py:68
  32.4 11.4 %while.26 = (s32[]{:T(128)}, f32[2,128,128]{2,1,0:T(8,128)S(1)}, s32[]{:T(128)}, s32[4]{0:T(128)S(1)}, bf16[4,128,128]{2,1,0:T(8,128)(2,1)S(1)}, /*index=5*/bf16...) while((s32[]{:T(128)}, f32[2,128,128]{2,1,0:T(8,128)S(1)}, ...), condition=%wide.region_2.3_spmd, body=%wide.region_0.2_spmd.sunk | while | flops 4227119 | bytes 197076 | solution.py:21
  45.0 84.1 %all-gather.1 = bf16[128,2,128]{2,1,0:T(2,128)(2,1)S(1)} all-gather(bf16[1,2,128]{2,1,0:T(2,128)(2,1)S(1)} %bitcast.113), channel_id=2, replica_groups=mesh['dom'=128,'feat'=4] {'dom'}, dimensions={0}, use_global_device_ids=true | all-gather | bytes 66048 | tf_op jit(solution)/shard_map/all_gather | solution.py:76
  131.7 2.7 scatter_fusion
  134.6 0.8 copy.53
  137.5 16.4 %reduce-scatter.4.cloned.1.call-done = bf16[128,256]{1,0:T(8,128)(2,1)} async-done(((bf16[512,256]{1,0:T(8,128)(2,1)}), bf16[128,256]{1,0:T(8,128)(2,1)}) %reduce-scatter.4.cloned.1.call-update) | async-done | bytes 65552
  153.9 1.0 copy.54
  155.6 9.1 %all_gather.7 = bf16[256,512]{1,0:T(8,128)(2,1)S(1)} all-gather(bf16[256,128]{1,0:T(8,128)(2,1)S(1)} %get-tuple-element.240), channel_id=1, replica_groups=mesh['dom'=128,'feat'=4] {'feat'}, dimensions={1}, use_global_device_ids=true | all-gather | bytes 327680 | tf_op jit(solution)/shard_map/all_gather | solution.py:92
  164.9 1.0 convolution_bitcast_fusion.2
  165.9 1.0 fusion.20
  166.9 0.9 convolution_bitcast_fusion.3
  167.8 11.5 %while.27 = (s32[]{:T(128)}, f32[2,128,128]{2,1,0:T(8,128)S(1)}, s32[]{:T(128)}, s32[4]{0:T(128)S(1)}, bf16[4,128,128]{2,1,0:T(8,128)(2,1)S(1)}, /*index=5*/bf16...) while((s32[]{:T(128)}, f32[2,128,128]{2,1,0:T(8,128)S(1)}, ...), condition=%wide.region_7.8_spmd, body=%wide.region_5.7_spmd.sunk | while | flops 4227119 | bytes 197076 | solution.py:37
  172.3 0.8 fusion.51
  177.8 0.8 fusion.51
  179.5 1.4 gather_fusion.2
  181.1 0.8 multiply_convert_fusion
  181.9 22.8 %all-to-all-start.1 = ((bf16[128,3,128]{2,1,0:T(4,128)(2,1)}), bf16[128,3,128]{2,1,0:T(4,128)(2,1)S(1)}, u32[]{:S(2)}, u32[]{:S(2)}) async-start(bf16[128,3,128]{2,1,0:T(4,128)(2,1)} %multiply_convert_fusion), calls=%async_computation.1 | async-start | bytes 262144 | tf_op jit(solution)/shard_map/all_to_all | solution.py:119
  204.7 248.5 %psum.31 = f32[128]{0:T(128)S(1)} all-reduce(f32[128]{0:T(128)S(1)} %get-tuple-element.239), channel_id=1, replica_groups=mesh['dom'=128,'feat'=4] {'dom'}, use_global_device_ids=true, to_apply=%region_14.15 | all-reduce | flops 128 | bytes 1024 | tf_op jit(solution)/shard_map/psum | solution.py:133
  453.7 73.0 %all-reduce.3.cloned.1.call-done = (f32[256,128]{1,0:T(8,128)}, f32[128,512]{0,1:T(8,128)}, f32[128,512]{0,1:T(8,128)}) async-done(((f32[256,128]{1,0:T(8,128)}, f32[128,512]{0,1:T(8,128)}, f32[128,512]{0,1:T(8,128)}), (f32[256,128]{1,0:T(8,128)}, f32[128,512]{0,1:T(8,128)}, f32[128,512]{0,1:T(8,128)})) %all-reduce.3.cloned.1.call-update) | async-done | bytes 655376 | tf_op jit(solution)/shard_map/psum | solution.py:128
  526.7 1.1 broadcast_multiply_fusion
  527.8 0.8 copy.48
  528.6 0.8 copy.49
  530.4 2.7 scatter_fusion.1
  (80 shorter events, 19.1 us)
Async XLA Ops:
  7.2 127.2 %copy-start = (bf16[128,512]{1,0:T(8,128)(2,1)S(1)}, bf16[128,512]{1,0:T(8,128)(2,1)}, u32[]{:S(2)}) copy-start(bf16[128,512]{1,0:T(8,128)(2,1)} %param.24) | copy-start | bytes 393220
  7.9 0.8 copy-start.1
  10.9 120.5 %all-to-all-start = ((bf16[128,3,128]{2,1,0:T(4,128)(2,1)}), bf16[128,3,128]{2,1,0:T(4,128)(2,1)S(1)}, u32[]{:S(2)}, u32[]{:S(2)}) async-start(bf16[128,3,128]{2,1,0:T(4,128)(2,1)} %reshape.243), calls=%async_computation | async-start | bytes 262144 | tf_op jit(solution)/shard_map/all_to_all | solution.py:68
  31.5 0.9 copy-start.2
  31.5 122.4 %reduce-scatter.4.cloned.1.call-start = ((), (), s32[]{:S(2)}) async-start(), calls=%async_computation.3 | async-start | bytes 327680
  31.5 0.8 copy-start.6
  31.5 0.8 copy-start.12
  43.8 0.7 copy-start.13
  43.8 85.3 %copy-start.3 = (bf16[256,256]{1,0:T(8,128)(2,1)S(1)}, bf16[256,256]{1,0:T(8,128)(2,1)}, u32[]{:S(2)}) copy-start(bf16[256,256]{1,0:T(8,128)(2,1)} %param.35) | copy-start | bytes 393220
  129.3 0.7 copy-start.8
  130.0 1.1 copy-start.4
  130.1 0.7 copy-start.10
  130.3 0.7 copy-start.9
  135.5 0.7 copy-start.7
  135.5 391.2 %all-reduce.3.cloned.1.call-start = ((), (), s32[]{:S(2)}) async-start(), calls=%async_computation.4 | async-start | bytes 1310720 | tf_op jit(solution)/shard_map/psum | solution.py:128
  136.3 0.7 copy-start.11
  153.9 1.0 copy-start.5
  181.9 348.4 %all-to-all-start.1 = ((bf16[128,3,128]{2,1,0:T(4,128)(2,1)}), bf16[128,3,128]{2,1,0:T(4,128)(2,1)S(1)}, u32[]{:S(2)}, u32[]{:S(2)}) async-start(bf16[128,3,128]{2,1,0:T(4,128)(2,1)} %multiply_convert_fusion), calls=%async_computation.1 | async-start | bytes 262144 | tf_op jit(solution)/shard_map/all_to_all | solution.py:119
Sparse Core Ops, SparseCore 0:
  135.6 18.2 reduce-scatter.3
  181.2 345.4 all-reduce.2
where the time goes:
time: 546 us; the launch traced here: 541 us
  blocking collectives  342 us (63%)
  waiting for transfers between devices  89.4 us (16%)
  starting transfers between devices  43.5 us (8%)
  local copies, waits for them, and re-layouts  16.2 us (3%)
  loops' own time  14.5 us (3%)
  between operations  14.4 us (3%)
  other arithmetic  13.8 us (3%)
  matrix products  7.1 us (1%)
    psum x1, blocking collectives, on_device(): lax.psum((grad_self_part, grad_neigh_part, bias_part), 'dom')  249 us
    all_gather x1, blocking collectives, on_device(): lax.all_gather(owned_rows, 'dom', axis=0, tiled=True)  84.1 us
    psum x1, waiting for transfers between devices, on_device(): every_hub = lax.psum(hub_term, 'dom')  73 us
    all_to_all x1, starting transfers between devices, on_device(): lax.all_to_all(returned.astype(jnp.bfloat16), 'dom', split_axis=0, concat...  22.8 us
    all_to_all x1, starting transfers between devices, on_device(): lax.all_to_all(outgoing, 'dom', split_axis=0, concat_axis=0, tiled=True)  20.6 us
    unnamed x3, waiting for transfers between devices  16.4 us
  transfers between devices with their start and end apart: 4, of which 2 were waited for; matrix products, arithmetic and copies ran while one was open for 2% of the time, Pallas kernels for 0%

commit v1 on v0

v1 whole, which is shorter than its diff:
```python
import math

import jax
import jax.numpy as jnp
from jax import lax
from jax.experimental import pallas as pl
from jax.experimental.pallas import tpu as pltpu
from jax.sharding import PartitionSpec as P

Z, Y, CORES, X = 16, 4, 2, 4
YC = Y * CORES
DOM = Z * YC
ROWS, W, TILE = 256, 128, 128
SLOTS, HUB, TMAX = 3, 2, 4
F32, BF16, I32 = jnp.float32, jnp.bfloat16, jnp.int32

ZROWS = 32
B_ROWS = SLOTS * Z + HUB * Z
C_ROWS = B_ROWS + 16

ST_A, ST_B, ST_P, ST_G, ST_C, ST_D, ST_RC, ST_RY, ST_RZ, ST_GZ, ST_GY, ST_GC = range(12)


def iota(shape, axis):
    return lax.broadcasted_iota(I32, shape, axis)


def dot(a, b):
    return jnp.dot(a, b, preferred_element_type=F32)


def dot_t(a, b):
    return lax.dot_general(a, b, (((1,), (1,)), ((), ())), preferred_element_type=F32)


def tdot(a, b):
    return lax.dot_general(a, b, (((0,), (0,)), ((), ())), preferred_element_type=F32)


def onehot(mask):
    return jnp.where(mask, 1.0, 0.0).astype(BF16)


def natural_to_plane():
    n, p = iota((DOM, DOM), 0), iota((DOM, DOM), 1)
    return onehot((n % YC == p // Z) & (n // YC == p % Z))


def hubs_to_plane():
    n, p = iota((DOM * HUB, DOM * HUB), 0), iota((DOM * HUB, DOM * HUB), 1)
    n2, p2 = n // HUB, p // HUB
    return onehot((n % HUB == p % HUB) & (n2 % YC == p2 // Z) & (n2 // YC == p2 % Z))


def hub_pick():
    q, n = iota((HUB * Z, 8 * Z), 0), iota((HUB * Z, 8 * Z), 1)
    return onehot((n // 8 == q // HUB) & (n % 8 == q % HUB))


def kernel(
    feat_h, wself_h, wneigh_h, bias_v, cot_h, tiles_h, pos_s, cnt_s, send_v, dest_v, gw_v, rc_v, hub_s, hw_h,
    out_h, gf_h, gs_h, gn_h, gb_h,
    feat, wself, wneigh, cot, tiles, hw,
    send_a, recv_a, send_b, recv_b, send_p, recv_p, gp, send_c, recv_c, send_d, recv_d,
    g_m, m_m, mt_m, base, pself, wg, rcore, ry, ysum, rz, wtot, out_v, gf_v, gb_v,
    in_sem, out_sem, send_sem, recv_sem,
):
    d = lax.axis_index("dom")
    f = lax.axis_index("feat")
    z, yc = d // YC, d % YC
    y, c = yc // CORES, yc % CORES

    def load(index, src, dst):
        copy = pltpu.make_async_copy(src, dst, in_sem.at[index])
        copy.start()
        return copy

    load_feat = load(0, feat_h, feat)
    load_tiles = load(1, tiles_h, tiles)
    load_hw = load(2, hw_h, hw)
    load_ws = load(3, wself_h, wself)
    load_wn = load(4, wneigh_h, wneigh)
    load_cot = load(5, cot_h, cot)

    def z_peer(k):
        return lax.rem(z + k, Z) * YC + yc

    def plane_peer(k):
        return z * YC + lax.rem(yc + k, YC)

    def y_peer(k):
        return z * YC + lax.rem(y + k, Y) * CORES + c

    partner = z * YC + y * CORES + (1 - c)

    def x_peer(k):
        return lax.rem(f + k, X)

    barrier = pltpu.get_barrier_semaphore()

    def greet(dom, feat_at):
        pl.semaphore_signal(barrier, inc=1, device_id=(dom, feat_at), device_id_type=pl.DeviceIdType.MESH)

    def loop(first, last, step):
        lax.fori_loop(first, last, lambda k, carry: (step(k), carry)[1], 0)

    loop(1, Z, lambda k: greet(z_peer(k), f))
    loop(1, YC, lambda k: greet(plane_peer(k), f))
    loop(1, X, lambda k: greet(d, x_peer(k)))

    def push(stage, src, dst, dom, feat_at):
        pltpu.make_async_remote_copy(
            src_ref=src,
            dst_ref=dst,
            send_sem=send_sem.at[stage],
            recv_sem=recv_sem.at[stage],
            device_id=(dom, feat_at),
            device_id_type=pl.DeviceIdType.MESH,
        ).start()

    def arrived(stage, ref):
        pltpu.make_async_copy(ref, ref, recv_sem.at[stage]).wait()

    def sent(stage, ref):
        pltpu.make_async_copy(ref, ref, send_sem.at[stage]).wait()

    row_of = iota((ROWS, DOM), 0)
    for s in range(SLOTS):
        g_m[:, s * DOM : (s + 1) * DOM] = onehot(row_of == send_v[s])
    lane8, sub8 = iota((8, ROWS), 1), iota((8, ROWS), 0)
    own_hub = onehot(((sub8 == 0) & (lane8 == hub_s[0, 0])) | ((sub8 == 1) & (lane8 == hub_s[0, 1])))
    load_feat.wait()
    groups = [tdot(g_m[:, s * DOM : (s + 1) * DOM], feat[...]).reshape(Z, YC, W) for s in range(SLOTS)]
    groups.append(jnp.broadcast_to(dot(own_hub, feat[...])[None], (Z, 8, W)))
    send_a[...] = jnp.concatenate(groups, axis=1).astype(BF16)

    pl.semaphore_wait(barrier, (Z - 1) + (YC - 1) + (X - 1))
    loop(1, Z, lambda k: push(ST_A, send_a.at[lax.rem(z + k, Z)], recv_a.at[z], z_peer(k), f))
    recv_a[pl.ds(z, 1)] = send_a[pl.ds(z, 1)]

    to_plane = natural_to_plane()
    pick = hub_pick()
    live = [jnp.where(rc_v[...] > s, gw_v[s], 0.0) for s in range(SLOTS)]
    packed = jnp.concatenate([dest_v[s].astype(F32) for s in range(SLOTS)] + live + [jnp.zeros((2, DOM), F32)], axis=0)
    packed = dot(packed.astype(BF16), to_plane)
    for s in range(SLOTS):
        dest_row = packed[s : s + 1].astype(I32)
        m_m[:, ROWS + s * DOM : ROWS + (s + 1) * DOM] = jnp.where(
            row_of == dest_row, packed[SLOTS + s : SLOTS + s + 1], 0.0
        ).astype(BF16)

    arrived(ST_A, recv_a.at[pl.ds(0, Z - 1)])
    got = recv_a[...].astype(F32)
    for s in range(SLOTS):
        part = got[:, s * YC : (s + 1) * YC].reshape(DOM, W).astype(BF16)
        send_b[:, s * Z : (s + 1) * Z] = tdot(to_plane, part).reshape(YC, Z, W).astype(BF16)
    hub_rows = dot(pick, got[:, SLOTS * YC :].reshape(Z * 8, W).astype(BF16))
    send_b[:, SLOTS * Z :] = jnp.broadcast_to(hub_rows[None], (YC, HUB * Z, W)).astype(BF16)
    loop(1, YC, lambda k: push(ST_B, send_b.at[lax.rem(yc + k, YC)], recv_b.at[yc], plane_peer(k), f))
    recv_b[pl.ds(yc, 1)] = send_b[pl.ds(yc, 1)]

    load_tiles.wait()
    tile_f32 = [tiles[0, t].astype(F32) for t in range(TMAX)]
    for k in range(4):
        block = jnp.zeros((TILE, TILE), F32)
        for t in range(TMAX):
            used = jnp.where((pos_s[0, t] == k) & (cnt_s[0] > t), 1.0, 0.0)
            block = block + used * tile_f32[t]
        m_m[(k // 2) * TILE : (k // 2 + 1) * TILE, (k % 2) * TILE : (k % 2 + 1) * TILE] = block.astype(BF16)
    load_hw.wait()
    m_m[:, ROWS + SLOTS * DOM :] = dot(hw[...], hubs_to_plane()).astype(BF16)
    base[...] = dot(m_m[:, :ROWS], feat[...])
    load_ws.wait()
    pself[...] = dot(feat[...], wself[...])
    load_wn.wait()

    arrived(ST_B, recv_b.at[pl.ds(0, YC - 1)])
    pulled = [recv_b[:, s * Z : (s + 1) * Z].reshape(DOM, W) for s in range(SLOTS)]
    pulled.append(recv_b[:, SLOTS * Z :].reshape(DOM * HUB, W))
    neigh = (base[...] + dot(m_m[:, ROWS:], jnp.concatenate(pulled, axis=0))).astype(BF16)
    partial = (pself[...] + dot(neigh, wneigh[...])).astype(BF16)
    for j in range(X):
        send_p[j] = partial[:, j * W : (j + 1) * W]
    loop(1, X, lambda k: push(ST_P, send_p.at[x_peer(k)], recv_p.at[f], d, x_peer(k)))
    recv_p[pl.ds(f, 1)] = send_p[pl.ds(f, 1)]

    mt_m[...] = m_m[...].T
    load_cot.wait()

    arrived(ST_P, recv_p.at[pl.ds(0, X - 1)])
    preact = jnp.sum(recv_p[...].astype(F32), axis=0) + bias_v[...].astype(F32)
    logistic = jax.nn.sigmoid(preact)
    out_v[...] = (preact * logistic).astype(BF16)
    grad_pre = (cot[...].astype(F32) * logistic * (1.0 + preact * (1.0 - logistic))).astype(BF16)
    gp[pl.ds(f, 1)] = grad_pre[None]
    loop(1, X, lambda k: push(ST_G, gp.at[f], gp.at[f], d, x_peer(k)))
    save_out = pltpu.make_async_copy(out_v, out_h, out_sem.at[0])
    save_out.start()
    bias_part = jnp.sum(grad_pre.astype(F32), axis=0, keepdims=True)

    arrived(ST_G, gp.at[pl.ds(0, X - 1)])
    gp_full = jnp.concatenate([gp[j] for j in range(X)], axis=1)
    neigh_grad = dot_t(gp_full, wneigh[...]).astype(BF16)
    back = dot(mt_m[...], neigh_grad)
    for s in range(SLOTS):
        at = ROWS + s * DOM
        send_c[:, s * Z : (s + 1) * Z] = back[at : at + DOM].reshape(YC, Z, W).astype(BF16)
    send_c[:, SLOTS * Z : B_ROWS] = back[ROWS + SLOTS * DOM :].reshape(YC, HUB * Z, W).astype(BF16)
    base[...] = back[:ROWS]

    def two_rows(row, first):
        high = row.astype(BF16).astype(F32)
        at = iota((8, W), 0)
        return jnp.where(at == first, high, jnp.where(at == first + 1, row - high, 0.0))

    bias_rows = jnp.concatenate([two_rows(bias_part, 0), jnp.zeros((8, W), F32)], axis=0)
    send_c[:, B_ROWS:] = jnp.broadcast_to(bias_rows[None], (YC, 16, W)).astype(BF16)
    loop(1, YC, lambda k: push(ST_C, send_c.at[lax.rem(yc + k, YC)], recv_c.at[yc], plane_peer(k), f))
    recv_c[pl.ds(yc, 1)] = send_c[pl.ds(yc, 1)]

    wg[0] = jnp.stack([tdot(feat[...], gp[j]) for j in range(X)])
    wg[1] = jnp.stack([tdot(neigh, gp[j]) for j in range(X)])
    push(ST_RC, wg.at[1 - c], rcore, partner, f)
    base[...] = base[...] + dot_t(gp_full, wself[...])

    arrived(ST_C, recv_c.at[pl.ds(0, YC - 1)])
    groups = []
    for s in range(SLOTS):
        part = recv_c[:, s * Z : (s + 1) * Z].reshape(DOM, W)
        groups.append(dot(to_plane, part).reshape(Z, YC, W))
    hub_sum = jnp.sum(recv_c[:, SLOTS * Z : B_ROWS].astype(F32), axis=0)
    bias_sum = jnp.sum(recv_c[:, B_ROWS:].astype(F32), axis=0)
    bias_sum = bias_sum[0:1] + bias_sum[1:2]
    tail = tdot(pick, hub_sum.astype(BF16)).reshape(Z, 8, W) + two_rows(bias_sum, HUB)[None]
    groups.append(tail)
    send_d[...] = jnp.concatenate(groups, axis=1).astype(BF16)
    loop(1, Z, lambda k: push(ST_D, send_d.at[lax.rem(z + k, Z)], recv_d.at[z], z_peer(k), f))
    recv_d[pl.ds(z, 1)] = send_d[pl.ds(z, 1)]

    arrived(ST_RC, rcore)
    rcore[...] = rcore[...] + wg[pl.ds(c, 1)].reshape(Y, W, W)
    loop(1, Y, lambda k: push(ST_RY, rcore.at[lax.rem(y + k, Y)], ry.at[y], y_peer(k), f))
    ry[pl.ds(y, 1)] = rcore[pl.ds(y, 1)]
    arrived(ST_RY, ry.at[pl.ds(0, Y - 1)])
    over_y = ry[0] + ry[1] + ry[2] + ry[3]
    ysum[...] = over_y

    loop(
        1,
        Z,
        lambda k: push(
            ST_RZ,
            ysum.at[pl.ds(pl.multiple_of(lax.rem(z + k, Z) * 8, 8), 8)],
            rz.at[z],
            z_peer(k),
            f,
        ),
    )
    mine = pl.ds(pl.multiple_of(z * 8, 8), 8)
    rz[pl.ds(z, 1)] = ysum[mine][None]

    arrived(ST_D, recv_d.at[pl.ds(0, Z - 1)])
    got = recv_d[...].astype(F32)
    pieces = [got[:, s * YC : (s + 1) * YC].reshape(DOM, W).astype(BF16) for s in range(SLOTS)]
    total = base[...] + dot(g_m[...], jnp.concatenate(pieces, axis=0))
    last = jnp.sum(got[:, SLOTS * YC :], axis=0)
    at_row = iota((ROWS, W), 0)
    for k in range(HUB):
        total = total + jnp.where(at_row == hub_s[0, k], last[k : k + 1], 0.0)
    gf_v[...] = total.astype(BF16)
    scale = 1.0 / math.sqrt(DOM * ROWS)
    gb_v[...] = (last[HUB : HUB + 1] + last[HUB + 1 : HUB + 2]) * scale
    save_gf = pltpu.make_async_copy(gf_v, gf_h, out_sem.at[1])
    save_gf.start()
    save_gb = pltpu.make_async_copy(gb_v, gb_h, out_sem.at[2])
    save_gb.start()

    arrived(ST_RZ, rz.at[pl.ds(0, Z - 1)])
    wtot[c, y, mine] = jnp.sum(rz[...], axis=0) * scale
    loop(1, Z, lambda k: push(ST_GZ, wtot.at[c, y, mine], wtot.at[c, y, mine], z_peer(k), f))
    arrived(ST_GZ, wtot.at[c, y, pl.ds(0, (Z - 1) * 8)])
    loop(1, Y, lambda k: push(ST_GY, wtot.at[c, y], wtot.at[c, y], y_peer(k), f))
    arrived(ST_GY, wtot.at[c, pl.ds(0, Y - 1)])
    push(ST_GC, wtot.at[c], wtot.at[c], partner, f)
    arrived(ST_GC, wtot.at[1 - c])
    saves = [save_out, save_gf, save_gb]
    for i, target in enumerate((gs_h, gn_h)):
        for j in range(X):
            copy = pltpu.make_async_copy(wtot.at[i, j], target.at[:, pl.ds(j * W, W)], out_sem.at[3 + i * X + j])
            copy.start()
            saves.append(copy)

    sent(ST_A, send_a.at[pl.ds(0, Z - 1)])
    sent(ST_B, send_b.at[pl.ds(0, YC - 1)])
    sent(ST_P, send_p.at[pl.ds(0, X - 1)])
    sent(ST_G, gp.at[pl.ds(0, X - 1)])
    sent(ST_C, send_c.at[pl.ds(0, YC - 1)])
    sent(ST_D, send_d.at[pl.ds(0, Z - 1)])
    sent(ST_RC, rcore)
    sent(ST_RY, ry.at[pl.ds(0, Y - 1)])
    sent(ST_RZ, rz.at[pl.ds(0, Z - 1)])
    sent(ST_GZ, rz.at[pl.ds(0, Z - 1)])
    sent(ST_GY, ry.at[pl.ds(0, Y - 1)])
    sent(ST_GC, rcore)
    for copy in saves:
        copy.wait()


def on_device(
    features, w_self, w_neigh, bias, cotangent, tile_vals, tile_pos, tile_count,
    send_rows, recv_dest, ghost_weight, recv_count, hub_rows, hub_weight,
):
    def by_slot(array):
        return jnp.transpose(array, (2, 0, 1))

    hbm = pl.BlockSpec(memory_space=pl.ANY)
    vmem = pl.BlockSpec(memory_space=pltpu.VMEM)
    smem = pl.BlockSpec(memory_space=pltpu.SMEM)
    cols = X * W
    rest = SLOTS * DOM + HUB * DOM
    output, grad_features, grad_self, grad_neigh, grad_bias = pl.pallas_call(
        kernel,
        out_shape=(
            jax.ShapeDtypeStruct((ROWS, W), BF16),
            jax.ShapeDtypeStruct((ROWS, W), BF16),
            jax.ShapeDtypeStruct((W, cols), F32),
            jax.ShapeDtypeStruct((W, cols), F32),
            jax.ShapeDtypeStruct((1, W), F32),
        ),
        in_specs=[hbm, hbm, hbm, vmem, hbm, hbm, smem, smem, vmem, vmem, vmem, vmem, smem, hbm],
        out_specs=(hbm,) * 5,
        scratch_shapes=[
            pltpu.VMEM((ROWS, W), BF16),
            pltpu.VMEM((W, cols), BF16),
            pltpu.VMEM((W, cols), BF16),
            pltpu.VMEM((ROWS, W), BF16),
            pltpu.VMEM((1, TMAX, TILE, TILE), BF16),
            pltpu.VMEM((ROWS, HUB * DOM), BF16),
            pltpu.VMEM((Z, ZROWS, W), BF16),
            pltpu.VMEM((Z, ZROWS, W), BF16),
            pltpu.VMEM((YC, B_ROWS, W), BF16),
            pltpu.VMEM((YC, B_ROWS, W), BF16),
            pltpu.VMEM((X, ROWS, W), BF16),
            pltpu.VMEM((X, ROWS, W), BF16),
            pltpu.VMEM((X, ROWS, W), BF16),
            pltpu.VMEM((YC, C_ROWS, W), BF16),
            pltpu.VMEM((YC, C_ROWS, W), BF16),
            pltpu.VMEM((Z, ZROWS, W), BF16),
            pltpu.VMEM((Z, ZROWS, W), BF16),
            pltpu.VMEM((ROWS, SLOTS * DOM), BF16),
            pltpu.VMEM((ROWS, ROWS + rest), BF16),
            pltpu.VMEM((ROWS + rest, ROWS), BF16),
            pltpu.VMEM((ROWS, W), F32),
            pltpu.VMEM((ROWS, cols), F32),
            pltpu.VMEM((2, Y, W, W), F32),
            pltpu.VMEM((Y, W, W), F32),
            pltpu.VMEM((Y, W, W), F32),
            pltpu.VMEM((W, W), F32),
            pltpu.VMEM((Z, 8, W), F32),
            pltpu.VMEM((2, Y, W, W), F32),
            pltpu.VMEM((ROWS, W), BF16),
            pltpu.VMEM((ROWS, W), BF16),
            pltpu.VMEM((1, W), F32),
            pltpu.SemaphoreType.DMA((6,)),
            pltpu.SemaphoreType.DMA((11,)),
            pltpu.SemaphoreType.DMA((12,)),
            pltpu.SemaphoreType.DMA((12,)),
        ],
        compiler_params=pltpu.CompilerParams(
            collective_id=0, has_side_effects=True, vmem_limit_bytes=32 * 1024 * 1024
        ),
    )(
        features, w_self, w_neigh, bias.reshape(1, W), cotangent, tile_vals, tile_pos, tile_count,
        by_slot(send_rows), by_slot(recv_dest), by_slot(ghost_weight), recv_count, hub_rows, hub_weight,
    )
    return output, grad_features, grad_self, grad_neigh, grad_bias.reshape(W)


def solution(mesh):
    placed = (
        P("dom", "feat"),
        P("feat", None),
        P("feat", None),
        P("feat"),
        P("dom", "feat"),
        P("dom", None, None, None),
        P("dom", None),
        P("dom"),
        P("dom", None, None),
        P("dom", None, None),
        P("dom", None, None),
        P("dom", None),
        P("dom", None),
        P("dom", None),
    )
    return jax.shard_map(
        on_device,
        mesh=mesh,
        in_specs=placed,
        out_specs=(P("dom", "feat"), P("dom", "feat"), P("feat", None), P("feat", None), P("feat")),
        check_vma=False,
    )
```

time: 546 us -> 86.3 us (0.16)
  blocking collectives: 342 us -> 0 us
  waiting for transfers between devices: 89.4 us -> 0 us
  Pallas kernels: 0 us -> 75.5 us
  starting transfers between devices: 43.5 us -> 0 us
  loops' own time: 14.5 us -> 0 us
  other arithmetic: 13.8 us -> 0 us
  between operations: 14.4 us -> 1.36 us
  matrix products: 7.1 us -> 0 us
  local copies, waits for them, and re-layouts: 16.2 us -> 9.17 us
    psum x1 -> x0, blocking collectives: 249 us -> none  [on_device(): lax.psum((grad_self_part, grad_neigh_part, bias_part), 'dom')]
    all_gather x2 -> x0, blocking collectives: 93.2 us -> none  [the longest x1 84.1 us: on_device(): lax.all_gather(owned_rows, 'dom', axis=0, tiled=True)]
    pallas_call x0 -> x1, Pallas kernels: none -> 75.5 us  [on_device(): pl.pallas_call(kernel, out_shape=(jax.ShapeDtypeStruct((ROWS, W), BF16),...]
    psum x1 -> x0, waiting for transfers between devices: 73 us -> none  [on_device(): every_hub = lax.psum(hub_term, 'dom')]
    all_to_all x2 -> x0, starting transfers between devices: 43.4 us -> none  [the longest x1 22.8 us: on_device(): lax.all_to_all(returned.astype(jnp.bfloat16), 'dom', split_axis=0, concat...]
    unnamed x3 -> x0, waiting for transfers between devices: 16.4 us -> none
    another operation x2 -> x0, loops' own time: 14.5 us -> none  [the longest x1 7.24 us: tile_forward(): lax.fori_loop(0, count_here, add_tile, jnp.zeros(blocks.shape, jnp.float32))]
    dot_general x12 -> x0, matrix products: 7.1 us -> none  [the longest x2 1.67 us: add_tile(): lax.dot_general(tiles_here[slot_index], blocks[tile_place // block_count]...]
  transfers between devices with their start and end apart: 4 -> 0, of which waited for: 2 -> 0; matrix products, arithmetic and copies ran while one was open for 2% -> 0% of each run, Pallas kernels for 0% -> 0%
where the time goes in v1:
time: 86.3 us; the launch traced here: 86 us
  Pallas kernels  75.5 us (87%)
  local copies, waits for them, and re-layouts  9.17 us (11%)
  between operations  1.36 us (2%)
    pallas_call x1, Pallas kernels, on_device(): pl.pallas_call(kernel, out_shape=(jax.ShapeDtypeStruct((ROWS, W), BF16),...  75.5 us
    unnamed x31, local copies, waits for them, and re-layouts  9.17 us

profile of v1, /device:TPU:1, one launch (start us, length us, event | category | flops | bytes accessed | tf_op | source)
XLA Modules:
  0.0 86.0 jit_solution(8474640457026005714)
XLA Ops:
  1.3 0.0 copy-start.11
  1.3 0.0 copy-start.12
  1.3 0.0 copy-start.8
  1.3 0.0 copy-start.10
  1.3 0.0 copy-start.6
  1.3 0.0 copy-start.7
  1.3 0.0 copy-start.9
  1.4 0.6 copy-done.11
  1.9 0.0 copy-done.12
  2.0 0.0 copy-done.8
  2.0 0.0 copy-done.6
  2.0 0.0 copy-done.7
  2.0 0.9 %copy-done = bf16[128,512]{1,0:T(8,128)(2,1)S(1)} copy-done((bf16[128,512]{1,0:T(8,128)(2,1)S(1)}, bf16[128,512]{1,0:T(8,128)(2,1)}, u32[]{:S(2)}) %copy-start) | copy-done | bytes 131096
  3.0 0.9 %copy-done.1 = bf16[128,512]{1,0:T(8,128)(2,1)S(1)} copy-done((bf16[128,512]{1,0:T(8,128)(2,1)S(1)}, bf16[128,512]{1,0:T(8,128)(2,1)}, u32[]{:S(2)}) %copy-start.1) | copy-done | bytes 131096
  3.9 0.9 %copy-done.2 = bf16[1,4,128,128]{3,2,1,0:T(8,128)(2,1)S(1)} copy-done((bf16[1,4,128,128]{3,2,1,0:T(8,128)(2,1)S(1)}, bf16[1,4,128,128]{3,2,1,0:T(8,128)(2,1)}, u32[]{:S(2)}) %copy-start.2) | copy-done | bytes 131096
  4.8 0.9 %copy-done.3 = bf16[256,256]{1,0:T(8,128)(2,1)S(1)} copy-done((bf16[256,256]{1,0:T(8,128)(2,1)S(1)}, bf16[256,256]{1,0:T(8,128)(2,1)}, u32[]{:S(2)}) %copy-start.3) | copy-done | bytes 131096
  5.7 0.8 copy-done.4
  6.5 0.8 copy-done.5
  7.3 75.5 %shard_map.173 = (bf16[256,128]{1,0:T(8,128)(2,1)S(1)}, bf16[256,128]{1,0:T(8,128)(2,1)S(1)}, f32[128,512]{1,0:T(8,128)S(1)}, f32[128,512]{1,0:T(8,128)S(1)}, f32[1,128]{1,0:T(1,128)S(1)}) custom-call(bf16[256,128]{1,0:T(8,128)(2,1)S(1)} %copy-done.4, bf16[128,512]{1,0:T(8,128)(2,1)S(1)} %copy-done, bf16[128,512]{1,0:T(8,128)(2,1)S(1)} %copy-done.1, ...), custom_call_target="tpu_custom_call" | custom-call | tf_op jit(solution)/shard_map/pallas_call | solution.py:321
  82.8 0.6 copy.25
  83.4 0.6 copy.26
  84.1 0.7 copy.27
  84.8 0.7 copy.28
  85.5 0.5 copy.29
  (8 shorter events, 0.0 us)
Async XLA Ops:
  1.3 0.7 copy-start.11
  1.3 0.7 copy-start.12
  1.3 0.7 copy-start.8
  1.3 0.7 copy-start.10
  1.3 0.7 copy-start.6
  1.3 0.7 copy-start.7
  1.3 0.7 copy-start.9
  2.0 0.9 %copy-start = (bf16[128,512]{1,0:T(8,128)(2,1)S(1)}, bf16[128,512]{1,0:T(8,128)(2,1)}, u32[]{:S(2)}) copy-start(bf16[128,512]{1,0:T(8,128)(2,1)} %wself_h.1) | copy-start | bytes 393220
  3.0 0.9 %copy-start.1 = (bf16[128,512]{1,0:T(8,128)(2,1)S(1)}, bf16[128,512]{1,0:T(8,128)(2,1)}, u32[]{:S(2)}) copy-start(bf16[128,512]{1,0:T(8,128)(2,1)} %wneigh_h.1) | copy-start | bytes 393220
  3.9 0.9 %copy-start.2 = (bf16[1,4,128,128]{3,2,1,0:T(8,128)(2,1)S(1)}, bf16[1,4,128,128]{3,2,1,0:T(8,128)(2,1)}, u32[]{:S(2)}) copy-start(bf16[1,4,128,128]{3,2,1,0:T(8,128)(2,1)} %tiles_h.1) | copy-start | bytes 393220
  4.8 0.9 %copy-start.3 = (bf16[256,256]{1,0:T(8,128)(2,1)S(1)}, bf16[256,256]{1,0:T(8,128)(2,1)}, u32[]{:S(2)}) copy-start(bf16[256,256]{1,0:T(8,128)(2,1)} %hw_h.1) | copy-start | bytes 393220
  5.7 0.8 copy-start.4
  6.5 0.8 copy-start.5

commit v2 on v1

--- a/solution.py
+++ b/solution.py
@@ -58,29 +58,35 @@
 
 
 def kernel(
-    feat_h, wself_h, wneigh_h, bias_v, cot_h, tiles_h, pos_s, cnt_s, send_v, dest_v, gw_v, rc_v, hub_s, hw_h,
-    out_h, gf_h, gs_h, gn_h, gb_h,
-    feat, wself, wneigh, cot, tiles, hw,
+    feat_h, wself_h, wneigh_h, bias_h, cot_h, tiles_h, pos_h, cnt_s, send_h, dest_h, gw_h, rc_h, hub_h, hw_h,
+    out_v, gf_v, wtot, gb_v,
+    feat, wself, wneigh, bias_v, cot, tiles, pos_s, send_v, dest_v, gw_v, rc_v, hub_s, hw,
     send_a, recv_a, send_b, recv_b, send_p, recv_p, gp, send_c, recv_c, send_d, recv_d,
-    g_m, m_m, mt_m, base, pself, wg, rcore, ry, ysum, rz, wtot, out_v, gf_v, gb_v,
-    in_sem, out_sem, send_sem, recv_sem,
+    g_m, m_m, mt_m, base, pself, wg, rcore, ry, ysum, rz,
+    in_sem, send_sem, recv_sem,
 ):
     d = lax.axis_index("dom")
     f = lax.axis_index("feat")
     z, yc = d // YC, d % YC
     y, c = yc // CORES, yc % CORES
 
-    def load(index, src, dst):
-        copy = pltpu.make_async_copy(src, dst, in_sem.at[index])
+    loads = []
+
+    def load(src, dst):
+        copy = pltpu.make_async_copy(src, dst, in_sem.at[len(loads)])
         copy.start()
+        loads.append(copy)
         return copy
 
-    load_feat = load(0, feat_h, feat)
-    load_tiles = load(1, tiles_h, tiles)
-    load_hw = load(2, hw_h, hw)
-    load_ws = load(3, wself_h, wself)
-    load_wn = load(4, wneigh_h, wneigh)
-    load_cot = load(5, cot_h, cot)
+    load_send = load(send_h, send_v)
+    load_hub = load(hub_h, hub_s)
+    load_feat = load(feat_h, feat)
+    load_edges = [load(dest_h, dest_v), load(gw_h, gw_v), load(rc_h, rc_v)]
+    load_tiles = [load(tiles_h, tiles), load(pos_h, pos_s)]
+    load_hw = load(hw_h, hw)
+    load_ws = load(wself_h, wself)
+    load_wn = load(wneigh_h, wneigh)
+    load_cot = [load(cot_h, cot), load(bias_h, bias_v)]
 
     def z_peer(k):
         return lax.rem(z + k, Z) * YC + yc
@@ -124,7 +130,11 @@
     def sent(stage, ref):
         pltpu.make_async_copy(ref, ref, send_sem.at[stage]).wait()
 
+    pending = []
+
     row_of = iota((ROWS, DOM), 0)
+    load_send.wait()
+    load_hub.wait()
     for s in range(SLOTS):
         g_m[:, s * DOM : (s + 1) * DOM] = onehot(row_of == send_v[s])
     lane8, sub8 = iota((8, ROWS), 1), iota((8, ROWS), 0)
@@ -136,10 +146,13 @@
 
     pl.semaphore_wait(barrier, (Z - 1) + (YC - 1) + (X - 1))
     loop(1, Z, lambda k: push(ST_A, send_a.at[lax.rem(z + k, Z)], recv_a.at[z], z_peer(k), f))
+    pending.append((ST_A, send_a.at[pl.ds(0, Z - 1)]))
     recv_a[pl.ds(z, 1)] = send_a[pl.ds(z, 1)]
 
     to_plane = natural_to_plane()
     pick = hub_pick()
+    for copy in load_edges:
+        copy.wait()
     live = [jnp.where(rc_v[...] > s, gw_v[s], 0.0) for s in range(SLOTS)]
     packed = jnp.concatenate([dest_v[s].astype(F32) for s in range(SLOTS)] + live + [jnp.zeros((2, DOM), F32)], axis=0)
     packed = dot(packed.astype(BF16), to_plane)
@@ -157,9 +170,11 @@
     hub_rows = dot(pick, got[:, SLOTS * YC :].reshape(Z * 8, W).astype(BF16))
     send_b[:, SLOTS * Z :] = jnp.broadcast_to(hub_rows[None], (YC, HUB * Z, W)).astype(BF16)
     loop(1, YC, lambda k: push(ST_B, send_b.at[lax.rem(yc + k, YC)], recv_b.at[yc], plane_peer(k), f))
+    pending.append((ST_B, send_b.at[pl.ds(0, YC - 1)]))
     recv_b[pl.ds(yc, 1)] = send_b[pl.ds(yc, 1)]
 
-    load_tiles.wait()
+    for copy in load_tiles:
+        copy.wait()
     tile_f32 = [tiles[0, t].astype(F32) for t in range(TMAX)]
     for k in range(4):
         block = jnp.zeros((TILE, TILE), F32)
@@ -182,10 +197,12 @@
     for j in range(X):
         send_p[j] = partial[:, j * W : (j + 1) * W]
     loop(1, X, lambda k: push(ST_P, send_p.at[x_peer(k)], recv_p.at[f], d, x_peer(k)))
+    pending.append((ST_P, send_p.at[pl.ds(0, X - 1)]))
     recv_p[pl.ds(f, 1)] = send_p[pl.ds(f, 1)]
 
     mt_m[...] = m_m[...].T
-    load_cot.wait()
+    for copy in load_cot:
+        copy.wait()
 
     arrived(ST_P, recv_p.at[pl.ds(0, X - 1)])
     preact = jnp.sum(recv_p[...].astype(F32), axis=0) + bias_v[...].astype(F32)
@@ -194,8 +211,7 @@
     grad_pre = (cot[...].astype(F32) * logistic * (1.0 + preact * (1.0 - logistic))).astype(BF16)
     gp[pl.ds(f, 1)] = grad_pre[None]
     loop(1, X, lambda k: push(ST_G, gp.at[f], gp.at[f], d, x_peer(k)))
-    save_out = pltpu.make_async_copy(out_v, out_h, out_sem.at[0])
-    save_out.start()
+    pending.append((ST_G, gp.at[pl.ds(0, X - 1)]))
     bias_part = jnp.sum(grad_pre.astype(F32), axis=0, keepdims=True)
 
     arrived(ST_G, gp.at[pl.ds(0, X - 1)])
@@ -216,11 +232,13 @@
     bias_rows = jnp.concatenate([two_rows(bias_part, 0), jnp.zeros((8, W), F32)], axis=0)
     send_c[:, B_ROWS:] = jnp.broadcast_to(bias_rows[None], (YC, 16, W)).astype(BF16)
     loop(1, YC, lambda k: push(ST_C, send_c.at[lax.rem(yc + k, YC)], recv_c.at[yc], plane_peer(k), f))
+    pending.append((ST_C, send_c.at[pl.ds(0, YC - 1)]))
     recv_c[pl.ds(yc, 1)] = send_c[pl.ds(yc, 1)]
 
     wg[0] = jnp.stack([tdot(feat[...], gp[j]) for j in range(X)])
     wg[1] = jnp.stack([tdot(neigh, gp[j]) for j in range(X)])
     push(ST_RC, wg.at[1 - c], rcore, partner, f)
+    pending.append((ST_RC, rcore))
     base[...] = base[...] + dot_t(gp_full, wself[...])
 
     arrived(ST_C, recv_c.at[pl.ds(0, YC - 1)])
@@ -235,11 +253,13 @@
     groups.append(tail)
     send_d[...] = jnp.concatenate(groups, axis=1).astype(BF16)
     loop(1, Z, lambda k: push(ST_D, send_d.at[lax.rem(z + k, Z)], recv_d.at[z], z_peer(k), f))
+    pending.append((ST_D, send_d.at[pl.ds(0, Z - 1)]))
     recv_d[pl.ds(z, 1)] = send_d[pl.ds(z, 1)]
 
     arrived(ST_RC, rcore)
     rcore[...] = rcore[...] + wg[pl.ds(c, 1)].reshape(Y, W, W)
     loop(1, Y, lambda k: push(ST_RY, rcore.at[lax.rem(y + k, Y)], ry.at[y], y_peer(k), f))
+    pending.append((ST_RY, ry.at[pl.ds(0, Y - 1)]))
     ry[pl.ds(y, 1)] = rcore[pl.ds(y, 1)]
     arrived(ST_RY, ry.at[pl.ds(0, Y - 1)])
     over_y = ry[0] + ry[1] + ry[2] + ry[3]
@@ -256,6 +276,7 @@
             f,
         ),
     )
+    pending.append((ST_RZ, rz.at[pl.ds(0, Z - 1)]))
     mine = pl.ds(pl.multiple_of(z * 8, 8), 8)
     rz[pl.ds(z, 1)] = ysum[mine][None]
 
@@ -270,39 +291,31 @@
     gf_v[...] = total.astype(BF16)
     scale = 1.0 / math.sqrt(DOM * ROWS)
     gb_v[...] = (last[HUB : HUB + 1] + last[HUB + 1 : HUB + 2]) * scale
-    save_gf = pltpu.make_async_copy(gf_v, gf_h, out_sem.at[1])
-    save_gf.start()
-    save_gb = pltpu.make_async_copy(gb_v, gb_h, out_sem.at[2])
-    save_gb.start()
 
     arrived(ST_RZ, rz.at[pl.ds(0, Z - 1)])
     wtot[c, y, mine] = jnp.sum(rz[...], axis=0) * scale
     loop(1, Z, lambda k: push(ST_GZ, wtot.at[c, y, mine], wtot.at[c, y, mine], z_peer(k), f))
+    pending.append((ST_GZ, rz.at[pl.ds(0, Z - 1)]))
     arrived(ST_GZ, wtot.at[c, y, pl.ds(0, (Z - 1) * 8)])
     loop(1, Y, lambda k: push(ST_GY, wtot.at[c, y], wtot.at[c, y], y_peer(k), f))
+    pending.append((ST_GY, ry.at[pl.ds(0, Y - 1)]))
     arrived(ST_GY, wtot.at[c, pl.ds(0, Y - 1)])
     push(ST_GC, wtot.at[c], wtot.at[c], partner, f)
+    pending.append((ST_GC, rcore))
     arrived(ST_GC, wtot.at[1 - c])
-    saves = [save_out, save_gf, save_gb]
+
+    for stage, ref in pending:
+        sent(stage, ref)
+
+
+def save_kernel(out_v, gf_v, wtot, gb_v, out_h, gf_h, gs_h, gn_h, gb_h, sem):
+    copies = [(out_v, out_h), (gf_v, gf_h), (gb_v, gb_h)]
     for i, target in enumerate((gs_h, gn_h)):
-        for j in range(X):
-            copy = pltpu.make_async_copy(wtot.at[i, j], target.at[:, pl.ds(j * W, W)], out_sem.at[3 + i * X + j])
-            copy.start()
-            saves.append(copy)
-
-    sent(ST_A, send_a.at[pl.ds(0, Z - 1)])
-    sent(ST_B, send_b.at[pl.ds(0, YC - 1)])
-    sent(ST_P, send_p.at[pl.ds(0, X - 1)])
-    sent(ST_G, gp.at[pl.ds(0, X - 1)])
-    sent(ST_C, send_c.at[pl.ds(0, YC - 1)])
-    sent(ST_D, send_d.at[pl.ds(0, Z - 1)])
-    sent(ST_RC, rcore)
-    sent(ST_RY, ry.at[pl.ds(0, Y - 1)])
-    sent(ST_RZ, rz.at[pl.ds(0, Z - 1)])
-    sent(ST_GZ, rz.at[pl.ds(0, Z - 1)])
-    sent(ST_GY, ry.at[pl.ds(0, Y - 1)])
-    sent(ST_GC, rcore)
-    for copy in saves:
+        copies += [(wtot.at[i, j], target.at[:, pl.ds(j * W, W)]) for j in range(X)]
+    copies = [pltpu.make_async_copy(src, dst, sem.at[i]) for i, (src, dst) in enumerate(copies)]
+    for copy in copies:
+        copy.start()
+    for copy in copies:
         copy.wait()
 
 
@@ -313,28 +326,33 @@
     def by_slot(array):
         return jnp.transpose(array, (2, 0, 1))
 
-    hbm = pl.BlockSpec(memory_space=pl.ANY)
+    hbm = pl.BlockSpec(memory_space=pltpu.HBM)
     vmem = pl.BlockSpec(memory_space=pltpu.VMEM)
-    smem = pl.BlockSpec(memory_space=pltpu.SMEM)
     cols = X * W
     rest = SLOTS * DOM + HUB * DOM
-    output, grad_features, grad_self, grad_neigh, grad_bias = pl.pallas_call(
+    results = pl.pallas_call(
         kernel,
         out_shape=(
             jax.ShapeDtypeStruct((ROWS, W), BF16),
             jax.ShapeDtypeStruct((ROWS, W), BF16),
-            jax.ShapeDtypeStruct((W, cols), F32),
-            jax.ShapeDtypeStruct((W, cols), F32),
+            jax.ShapeDtypeStruct((2, Y, W, W), F32),
             jax.ShapeDtypeStruct((1, W), F32),
         ),
-        in_specs=[hbm, hbm, hbm, vmem, hbm, hbm, smem, smem, vmem, vmem, vmem, vmem, smem, hbm],
-        out_specs=(hbm,) * 5,
+        in_specs=[hbm] * 7 + [pl.BlockSpec(memory_space=pltpu.SMEM)] + [hbm] * 6,
+        out_specs=(vmem,) * 4,
         scratch_shapes=[
             pltpu.VMEM((ROWS, W), BF16),
             pltpu.VMEM((W, cols), BF16),
             pltpu.VMEM((W, cols), BF16),
+            pltpu.VMEM((1, W), BF16),
             pltpu.VMEM((ROWS, W), BF16),
             pltpu.VMEM((1, TMAX, TILE, TILE), BF16),
+            pltpu.SMEM((1, TMAX), I32),
+            pltpu.VMEM((SLOTS, 1, DOM), I32),
+            pltpu.VMEM((SLOTS, 1, DOM), I32),
+            pltpu.VMEM((SLOTS, 1, DOM), F32),
+            pltpu.VMEM((1, DOM), I32),
+            pltpu.SMEM((1, HUB), I32),
             pltpu.VMEM((ROWS, HUB * DOM), BF16),
             pltpu.VMEM((Z, ZROWS, W), BF16),
             pltpu.VMEM((Z, ZROWS, W), BF16),
@@ -357,12 +375,7 @@
             pltpu.VMEM((Y, W, W), F32),
             pltpu.VMEM((W, W), F32),
             pltpu.VMEM((Z, 8, W), F32),
-            pltpu.VMEM((2, Y, W, W), F32),
-            pltpu.VMEM((ROWS, W), BF16),
-            pltpu.VMEM((ROWS, W), BF16),
-            pltpu.VMEM((1, W), F32),
-            pltpu.SemaphoreType.DMA((6,)),
-            pltpu.SemaphoreType.DMA((11,)),
+            pltpu.SemaphoreType.DMA((13,)),
             pltpu.SemaphoreType.DMA((12,)),
             pltpu.SemaphoreType.DMA((12,)),
         ],
@@ -370,9 +383,27 @@
             collective_id=0, has_side_effects=True, vmem_limit_bytes=32 * 1024 * 1024
         ),
     )(
-        features, w_self, w_neigh, bias.reshape(1, W), cotangent, tile_vals, tile_pos, tile_count,
-        by_slot(send_rows), by_slot(recv_dest), by_slot(ghost_weight), recv_count, hub_rows, hub_weight,
+        *(
+            array if array is tile_count else pltpu.with_memory_space_constraint(array, pltpu.HBM)
+            for array in (
+                features, w_self, w_neigh, bias.reshape(1, W), cotangent, tile_vals, tile_pos, tile_count,
+                by_slot(send_rows), by_slot(recv_dest), by_slot(ghost_weight), recv_count, hub_rows, hub_weight,
+            )
+        )
     )
+    output, grad_features, grad_self, grad_neigh, grad_bias = pl.pallas_call(
+        save_kernel,
+        out_shape=(
+            jax.ShapeDtypeStruct((ROWS, W), BF16),
+            jax.ShapeDtypeStruct((ROWS, W), BF16),
+            jax.ShapeDtypeStruct((W, cols), F32),
+            jax.ShapeDtypeStruct((W, cols), F32),
+            jax.ShapeDtypeStruct((1, W), F32),
+        ),
+        in_specs=[vmem] * 4,
+        out_specs=(hbm,) * 5,
+        scratch_shapes=[pltpu.SemaphoreType.DMA((3 + 2 * X,))],
+    )(*results)
     return output, grad_features, grad_self, grad_neigh, grad_bias.reshape(W)
 
 

time: 86.3 us -> 80 us (0.927)
  local copies, waits for them, and re-layouts: 9.17 us -> 2.59 us
    unnamed x31 -> x8, local copies, waits for them, and re-layouts: 9.17 us -> 2.59 us
    pallas_call x0 -> x1, Pallas kernels: none -> 2.04 us  [on_device(): pl.pallas_call(save_kernel, out_shape=(jax.ShapeDtypeStruct((ROWS, W), BF...]
    pallas_call x1, Pallas kernels: 75.5 us -> 73.9 us  [on_device(): pl.pallas_call(kernel, out_shape=(jax.ShapeDtypeStruct((ROWS, W), BF16),...]
where the time goes in v2:
time: 80 us; the launch traced here: 79.8 us
  Pallas kernels  75.9 us (95%)
  local copies, waits for them, and re-layouts  2.59 us (3%)
  between operations  1.3 us (2%)
    pallas_call x1, Pallas kernels, on_device(): pl.pallas_call(kernel, out_shape=(jax.ShapeDtypeStruct((ROWS, W), BF16),...  73.9 us
    unnamed x8, local copies, waits for them, and re-layouts  2.59 us
    pallas_call x1, Pallas kernels, on_device(): pl.pallas_call(save_kernel, out_shape=(jax.ShapeDtypeStruct((ROWS, W), BF...  2.04 us

profile of v2, /device:TPU:1, one launch (start us, length us, event | category | flops | bytes accessed | tf_op | source)
XLA Modules:
  0.0 79.8 jit_solution(9383208906096540636)
XLA Ops:
  1.3 73.9 %shard_map.173 = (bf16[256,128]{1,0:T(8,128)(2,1)S(1)}, bf16[256,128]{1,0:T(8,128)(2,1)S(1)}, f32[2,4,128,128]{3,2,1,0:T(8,128)S(1)}, f32[1,128]{1,0:T(1,128)S(1)}) custom-call(bf16[256,128]{1,0:T(8,128)(2,1)} %feat_h.1, bf16[128,512]{1,0:T(8,128)(2,1)} %wself_h.1, bf16[128,512]{1,0:T(8,128)(2,1)} %wneigh_h.1, bf16[1,128]{1,0:T(2,128)(2,1)} %bitcast.8, ...), custom_call_target="tpu_custom_call" | custom-call | tf_op jit(solution)/shard_map/pallas_call | solution.py:333
  75.2 0.0 copy-start
  75.2 0.8 copy-done
  76.0 0.0 copy-start.1
  76.0 0.6 copy-done.1
  76.6 0.0 copy-start.2
  76.6 0.6 copy-done.2
  77.2 0.0 copy-start.3
  77.2 0.6 copy-done.3
  77.8 2.0 %shard_map.174 = (bf16[256,128]{1,0:T(8,128)(2,1)}, bf16[256,128]{1,0:T(8,128)(2,1)}, f32[128,512]{1,0:T(8,128)}, f32[128,512]{1,0:T(8,128)}, f32[1,128]{1,0:T(1,128)}) custom-call(bf16[256,128]{1,0:T(8,128)(2,1)} %copy-done.1, bf16[256,128]{1,0:T(8,128)(2,1)} %copy-done.2, f32[2,4,128,128]{3,2,1,0:T(8,128)} %copy-done, f32[1,128]{1,0:T(1,128)} %copy-done.3), custom_call_target="tpu_custom_call" | custom-call | tf_op jit(solution)/shard_map/pallas_call | solution.py:394
Async XLA Ops:
  75.2 0.8 copy-start
  76.0 0.6 copy-start.1
  76.6 0.6 copy-start.2
  77.2 0.6 copy-start.3

commit v3 on v2

v3 whole, which is shorter than its diff:
```python
import math

import jax
import jax.numpy as jnp
from jax import lax
from jax.experimental import pallas as pl
from jax.experimental.pallas import tpu as pltpu
from jax.sharding import PartitionSpec as P

Z, Y, CORES, X = 16, 4, 2, 4
YC = Y * CORES
DOM = Z * YC
ROWS, W, TILE = 256, 128, 128
SLOTS, HUB, TMAX = 3, 2, 4
F32, BF16, I32 = jnp.float32, jnp.bfloat16, jnp.int32

ZROWS = 32
B_ROWS = SLOTS * Z + HUB * Z
C_ROWS = B_ROWS + 16
COT_ROWS = ROWS + 16

(ST_A, ST_B, ST_XF, ST_XW, ST_XC, ST_CW, ST_P, ST_C, ST_D, ST_RC, ST_RY, ST_RZ, ST_GZ, ST_GC, ST_GY) = range(15)
STAGES = ST_GY + Y


def iota(shape, axis):
    return lax.broadcasted_iota(I32, shape, axis)


def dot(a, b):
    return jnp.dot(a, b, preferred_element_type=F32)


def dot_t(a, b):
    return lax.dot_general(a, b, (((1,), (1,)), ((), ())), preferred_element_type=F32)


def tdot(a, b):
    return lax.dot_general(a, b, (((0,), (0,)), ((), ())), preferred_element_type=F32)


def onehot(mask):
    return jnp.where(mask, 1.0, 0.0).astype(BF16)


def natural_to_plane():
    n, p = iota((DOM, DOM), 0), iota((DOM, DOM), 1)
    return onehot((n % YC == p // Z) & (n // YC == p % Z))


def hubs_to_plane():
    n, p = iota((DOM * HUB, DOM * HUB), 0), iota((DOM * HUB, DOM * HUB), 1)
    n2, p2 = n // HUB, p // HUB
    return onehot((n % HUB == p % HUB) & (n2 % YC == p2 // Z) & (n2 // YC == p2 % Z))


def hub_pick():
    q, n = iota((HUB * Z, 8 * Z), 0), iota((HUB * Z, 8 * Z), 1)
    return onehot((n // 8 == q // HUB) & (n % 8 == q % HUB))


def kernel(
    feat_h, wself_h, wneigh_h, bias_h, cot_h, tiles_h, pos_h, cnt_s, send_h, dest_h, gw_h, rc_h, hub_h, hw_h,
    out_v, gf_v, wtot, gb_v,
    feat_x, w_x, cot_x, neigh_x, bias_v, tiles, pos_s, send_v, dest_v, gw_v, rc_v, hub_s, hw,
    send_a, recv_a, send_b, recv_b, gp, own_pre, send_c, recv_c, send_d, recv_d,
    g_m, m_m, mt_m, base, pself, wsend, wown, rcore, send_ry, ry, ysum, rz, gz,
    in_sem, send_sem, recv_sem,
):
    d = lax.axis_index("dom")
    f = lax.axis_index("feat")
    z, yc = d // YC, d % YC
    y, c = yc // CORES, yc % CORES
    partner = z * YC + y * CORES + (1 - c)

    def z_peer(k):
        return lax.rem(z + k, Z) * YC + yc

    def plane_peer(k):
        return z * YC + lax.rem(yc + k, YC)

    def y_peer(k):
        return z * YC + lax.rem(y + k, Y) * CORES + c

    def x_peer(k):
        return lax.rem(f + k, X)

    def around(count, step):
        def body(i, carry):
            half = (i + 1) // 2
            step(count // 2 + jnp.where(i % 2 == 1, -half, half))
            return carry

        lax.fori_loop(0, count - 1, body, 0)

    barrier = pltpu.get_barrier_semaphore()

    def greet(dom, feat_at):
        pl.semaphore_signal(barrier, inc=1, device_id=(dom, feat_at), device_id_type=pl.DeviceIdType.MESH)

    around(Z, lambda k: greet(z_peer(k), f))
    around(YC, lambda k: greet(plane_peer(k), f))
    around(X, lambda k: greet(d, x_peer(k)))

    loads = []

    def load(src, dst):
        copy = pltpu.make_async_copy(src, dst, in_sem.at[len(loads)])
        copy.start()
        loads.append(copy)
        return copy

    load_send = load(send_h, send_v)
    load_hub = load(hub_h, hub_s)
    load_feat = load(feat_h, feat_x.at[f])
    load_w = [load(wself_h, w_x.at[0, f]), load(wneigh_h, w_x.at[1, f])]
    load_cot = [load(cot_h, cot_x.at[f, pl.ds(0, ROWS)]), load(bias_h, bias_v)]
    load_edges = [load(dest_h, dest_v), load(gw_h, gw_v), load(rc_h, rc_v)]
    load_tiles = [load(tiles_h, tiles), load(pos_h, pos_s)]
    load_hw = load(hw_h, hw)

    def push(stage, src, dst, dom, feat_at):
        pltpu.make_async_remote_copy(
            src_ref=src,
            dst_ref=dst,
            send_sem=send_sem.at[stage],
            recv_sem=recv_sem.at[stage],
            device_id=(dom, feat_at),
            device_id_type=pl.DeviceIdType.MESH,
        ).start()

    def arrived(stage, ref):
        pltpu.make_async_copy(ref, ref, recv_sem.at[stage]).wait()

    def sent(stage, ref):
        pltpu.make_async_copy(ref, ref, send_sem.at[stage]).wait()

    pending = []

    row_of = iota((ROWS, DOM), 0)
    load_send.wait()
    load_hub.wait()
    for s in range(SLOTS):
        g_m[:, s * DOM : (s + 1) * DOM] = onehot(row_of == send_v[s])
    lane8, sub8 = iota((8, ROWS), 1), iota((8, ROWS), 0)
    own_hub = onehot(((sub8 == 0) & (lane8 == hub_s[0, 0])) | ((sub8 == 1) & (lane8 == hub_s[0, 1])))
    load_feat.wait()
    feat = feat_x[f]
    groups = [tdot(g_m[:, s * DOM : (s + 1) * DOM], feat).reshape(Z, YC, W) for s in range(SLOTS)]
    groups.append(jnp.broadcast_to(dot(own_hub, feat)[None], (Z, 8, W)))
    send_a[...] = jnp.concatenate(groups, axis=1).astype(BF16)

    pl.semaphore_wait(barrier, (Z - 1) + (YC - 1) + (X - 1))
    around(Z, lambda k: push(ST_A, send_a.at[lax.rem(z + k, Z)], recv_a.at[z], z_peer(k), f))
    pending.append((ST_A, send_a.at[pl.ds(0, Z - 1)]))
    recv_a[pl.ds(z, 1)] = send_a[pl.ds(z, 1)]

    around(X, lambda k: push(ST_XF, feat_x.at[f], feat_x.at[f], d, x_peer(k)))
    pending.append((ST_XF, feat_x.at[pl.ds(0, X - 1)]))
    for copy in load_w:
        copy.wait()
    around(X, lambda k: push(ST_XW, w_x.at[c, f], w_x.at[c, f], d, x_peer(k)))
    pending.append((ST_XW, w_x.at[0, pl.ds(0, X - 1)]))
    for copy in load_cot:
        copy.wait()
    bias_rows = jnp.concatenate([bias_v[...].astype(F32), jnp.zeros((15, W), F32)], axis=0)
    cot_x[pl.ds(f, 1), ROWS:] = bias_rows.astype(BF16)[None]
    around(X, lambda k: push(ST_XC, cot_x.at[f], cot_x.at[f], d, x_peer(k)))
    pending.append((ST_XC, cot_x.at[pl.ds(0, X - 1)]))

    to_plane = natural_to_plane()
    pick = hub_pick()
    for copy in load_edges:
        copy.wait()
    live = [jnp.where(rc_v[...] > s, gw_v[s], 0.0) for s in range(SLOTS)]
    packed = jnp.concatenate([dest_v[s].astype(F32) for s in range(SLOTS)] + live + [jnp.zeros((2, DOM), F32)], axis=0)
    packed = dot(packed.astype(BF16), to_plane)
    for s in range(SLOTS):
        dest_row = packed[s : s + 1].astype(I32)
        m_m[:, ROWS + s * DOM : ROWS + (s + 1) * DOM] = jnp.where(
            row_of == dest_row, packed[SLOTS + s : SLOTS + s + 1], 0.0
        ).astype(BF16)

    arrived(ST_A, recv_a.at[pl.ds(0, Z - 1)])
    got = recv_a[...].astype(F32)
    for s in range(SLOTS):
        part = got[:, s * YC : (s + 1) * YC].reshape(DOM, W).astype(BF16)
        send_b[:, s * Z : (s + 1) * Z] = tdot(to_plane, part).reshape(YC, Z, W).astype(BF16)
    hub_rows = dot(pick, got[:, SLOTS * YC :].reshape(Z * 8, W).astype(BF16))
    send_b[:, SLOTS * Z :] = jnp.broadcast_to(hub_rows[None], (YC, HUB * Z, W)).astype(BF16)
    around(YC, lambda k: push(ST_B, send_b.at[lax.rem(yc + k, YC)], recv_b.at[yc], plane_peer(k), f))
    pending.append((ST_B, send_b.at[pl.ds(0, YC - 1)]))
    recv_b[pl.ds(yc, 1)] = send_b[pl.ds(yc, 1)]

    for copy in load_tiles:
        copy.wait()
    tile_f32 = [tiles[0, t].astype(F32) for t in range(TMAX)]
    for k in range(4):
        block = jnp.zeros((TILE, TILE), F32)
        for t in range(TMAX):
            used = jnp.where((pos_s[0, t] == k) & (cnt_s[0] > t), 1.0, 0.0)
            block = block + used * tile_f32[t]
        m_m[(k // 2) * TILE : (k // 2 + 1) * TILE, (k % 2) * TILE : (k % 2 + 1) * TILE] = block.astype(BF16)
    load_hw.wait()
    m_m[:, ROWS + SLOTS * DOM :] = dot(hw[...], hubs_to_plane()).astype(BF16)
    base[...] = dot(m_m[:, :ROWS], feat_x[f])

    arrived(ST_B, recv_b.at[pl.ds(0, YC - 1)])
    pulled = [recv_b[:, s * Z : (s + 1) * Z].reshape(DOM, W) for s in range(SLOTS)]
    pulled.append(recv_b[:, SLOTS * Z :].reshape(DOM * HUB, W))
    neigh = (base[...] + dot(m_m[:, ROWS:], jnp.concatenate(pulled, axis=0))).astype(BF16)
    neigh_x[pl.ds(f, 1)] = neigh[None]
    around(X, lambda k: push(ST_P, neigh_x.at[f], neigh_x.at[f], d, x_peer(k)))
    pending.append((ST_P, neigh_x.at[pl.ds(0, X - 1)]))

    arrived(ST_XW, w_x.at[0, pl.ds(0, X - 1)])
    around(X, lambda k: push(ST_CW, w_x.at[c, x_peer(k)], w_x.at[c, x_peer(k)], partner, f))
    pending.append((ST_CW, w_x.at[0, pl.ds(0, X - 1)]))
    mt_m[...] = m_m[...].T
    arrived(ST_XF, feat_x.at[pl.ds(0, X - 1)])
    arrived(ST_XC, cot_x.at[pl.ds(0, X - 1)])
    arrived(ST_CW, w_x.at[0, pl.ds(0, X - 1)])
    feat_full = jnp.concatenate([feat_x[j] for j in range(X)], axis=1)
    pself[...] = dot(feat_full, w_x[0].reshape(X * W, X * W))

    arrived(ST_P, neigh_x.at[pl.ds(0, X - 1)])
    neigh_full = jnp.concatenate([neigh_x[j] for j in range(X)], axis=1)
    for j in range(X):
        cols = slice(j * W, (j + 1) * W)
        w_cols = jnp.concatenate([w_x[1, i, :, cols] for i in range(X)], axis=0)
        bias_row = cot_x[j, ROWS : ROWS + 16].astype(F32)[0:1]
        preact = pself[:, cols] + dot(neigh_full, w_cols) + bias_row
        own_pre[j] = preact
        logistic = jax.nn.sigmoid(preact)
        gp[j] = (cot_x[j, :ROWS].astype(F32) * logistic * (1.0 + preact * (1.0 - logistic))).astype(BF16)

    first = c == 0
    rows_out = jnp.where(first, neigh_x[f], feat_x[f])
    for j in range(X):
        wsend[j] = tdot(rows_out, gp[j])
    push(ST_RC, wsend, rcore, partner, f)
    pending.append((ST_RC, rcore))
    rows_own = jnp.where(first, feat_x[f], neigh_x[f])
    for j in range(X):
        wown[j] = tdot(rows_own, gp[j])

    gp_full = jnp.concatenate([gp[j] for j in range(X)], axis=1)
    neigh_grad = dot_t(gp_full, w_x[1, f]).astype(BF16)
    back = dot(mt_m[...], neigh_grad)
    for s in range(SLOTS):
        at = ROWS + s * DOM
        send_c[:, s * Z : (s + 1) * Z] = back[at : at + DOM].reshape(YC, Z, W).astype(BF16)
    send_c[:, SLOTS * Z : B_ROWS] = back[ROWS + SLOTS * DOM :].reshape(YC, HUB * Z, W).astype(BF16)

    def two_rows(row, first):
        high = row.astype(BF16).astype(F32)
        at = iota((8, W), 0)
        return jnp.where(at == first, high, jnp.where(at == first + 1, row - high, 0.0))

    bias_part = jnp.sum(gp[f].astype(F32), axis=0, keepdims=True)
    bias_rows = jnp.concatenate([two_rows(bias_part, 0), jnp.zeros((8, W), F32)], axis=0)
    send_c[:, B_ROWS:] = jnp.broadcast_to(bias_rows[None], (YC, 16, W)).astype(BF16)
    around(YC, lambda k: push(ST_C, send_c.at[lax.rem(yc + k, YC)], recv_c.at[yc], plane_peer(k), f))
    pending.append((ST_C, send_c.at[pl.ds(0, YC - 1)]))
    recv_c[pl.ds(yc, 1)] = send_c[pl.ds(yc, 1)]

    arrived(ST_RC, rcore)
    send_ry[...] = (rcore[...] + wown[...]).astype(BF16)
    around(Y, lambda k: push(ST_RY, send_ry.at[lax.rem(y + k, Y)], ry.at[y], y_peer(k), f))
    pending.append((ST_RY, ry.at[pl.ds(0, Y - 1)]))
    ry[pl.ds(y, 1)] = send_ry[pl.ds(y, 1)]
    base[...] = back[:ROWS] + dot_t(gp_full, w_x[0, f])

    arrived(ST_RY, ry.at[pl.ds(0, Y - 1)])
    ysum[...] = jnp.sum(ry[...].astype(F32), axis=0)
    around(
        Z,
        lambda k: push(
            ST_RZ, ysum.at[pl.ds(pl.multiple_of(lax.rem(z + k, Z) * 8, 8), 8)], rz.at[z], z_peer(k), f
        ),
    )
    pending.append((ST_RZ, rz.at[pl.ds(0, Z - 1)]))
    mine = pl.ds(pl.multiple_of(z * 8, 8), 8)
    rz[pl.ds(z, 1)] = ysum[mine][None]

    arrived(ST_C, recv_c.at[pl.ds(0, YC - 1)])
    groups = []
    for s in range(SLOTS):
        part = recv_c[:, s * Z : (s + 1) * Z].reshape(DOM, W)
        groups.append(dot(to_plane, part).reshape(Z, YC, W))
    hub_sum = jnp.sum(recv_c[:, SLOTS * Z : B_ROWS].astype(F32), axis=0)
    bias_sum = jnp.sum(recv_c[:, B_ROWS:].astype(F32), axis=0)
    bias_sum = bias_sum[0:1] + bias_sum[1:2]
    groups.append(tdot(pick, hub_sum.astype(BF16)).reshape(Z, 8, W) + two_rows(bias_sum, HUB)[None])
    send_d[...] = jnp.concatenate(groups, axis=1).astype(BF16)
    around(Z, lambda k: push(ST_D, send_d.at[lax.rem(z + k, Z)], recv_d.at[z], z_peer(k), f))
    pending.append((ST_D, send_d.at[pl.ds(0, Z - 1)]))
    recv_d[pl.ds(z, 1)] = send_d[pl.ds(z, 1)]
    preact = own_pre[f]
    out_v[...] = (preact * jax.nn.sigmoid(preact)).astype(BF16)

    arrived(ST_RZ, rz.at[pl.ds(0, Z - 1)])
    scale = 1.0 / math.sqrt(DOM * ROWS)
    gz[mine] = jnp.sum(rz[...], axis=0) * scale
    around(Z, lambda k: push(ST_GZ, gz.at[mine], gz.at[mine], z_peer(k), f))
    pending.append((ST_GZ, rz.at[pl.ds(0, Z - 1)]))

    arrived(ST_D, recv_d.at[pl.ds(0, Z - 1)])
    got = recv_d[...].astype(F32)
    pieces = [got[:, s * YC : (s + 1) * YC].reshape(DOM, W).astype(BF16) for s in range(SLOTS)]
    total = base[...] + dot(g_m[...], jnp.concatenate(pieces, axis=0))
    last = jnp.sum(got[:, SLOTS * YC :], axis=0)
    at_row = iota((ROWS, W), 0)
    for k in range(HUB):
        total = total + jnp.where(at_row == hub_s[0, k], last[k : k + 1], 0.0)
    gf_v[...] = total.astype(BF16)
    gb_v[...] = (last[HUB : HUB + 1] + last[HUB + 1 : HUB + 2]) * scale

    arrived(ST_GZ, gz.at[pl.ds(0, (Z - 1) * 8)])
    wtot[c, y] = gz[...].astype(BF16)
    for k in (2, 1, 3):
        push(ST_GY + k, wtot.at[c, y], wtot.at[c, y], y_peer(k), f)
        pending.append((ST_GY + k, wtot.at[0, 0]))
    push(ST_GC, wtot.at[c, y], wtot.at[c, y], partner, f)
    for k in (1, 3, 2):
        source = lax.rem(y + Y - k, Y)
        arrived(ST_GY + k, wtot.at[c, source])
        push(ST_GC, wtot.at[c, source], wtot.at[c, source], partner, f)
    pending.append((ST_GC, wtot.at[0]))
    arrived(ST_GC, wtot.at[1 - c])
    for stage, ref in pending:
        sent(stage, ref)


def save_kernel(out_v, gf_v, wtot, gb_v, out_h, gf_h, gs_h, gn_h, gb_h, gs_v, gn_v, sem):
    copies = []

    def save(src, dst):
        copies.append(pltpu.make_async_copy(src, dst, sem.at[len(copies)]))
        copies[-1].start()

    save(out_v, out_h)
    save(gf_v, gf_h)
    save(gb_v, gb_h)
    for i, (wide, target) in enumerate(((gs_v, gs_h), (gn_v, gn_h))):
        for j in range(X):
            wide[:, j * W : (j + 1) * W] = wtot[i, j].astype(F32)
        save(wide, target)
    for copy in copies:
        copy.wait()


def on_device(
    features, w_self, w_neigh, bias, cotangent, tile_vals, tile_pos, tile_count,
    send_rows, recv_dest, ghost_weight, recv_count, hub_rows, hub_weight,
):
    def by_slot(array):
        return jnp.transpose(array, (2, 0, 1))

    hbm = pl.BlockSpec(memory_space=pltpu.HBM)
    vmem = pl.BlockSpec(memory_space=pltpu.VMEM)
    smem = pl.BlockSpec(memory_space=pltpu.SMEM)
    cols = X * W
    rest = SLOTS * DOM + HUB * DOM
    results = pl.pallas_call(
        kernel,
        out_shape=(
            pltpu.VMEM((ROWS, W), BF16),
            pltpu.VMEM((ROWS, W), BF16),
            pltpu.VMEM((2, Y, W, W), BF16),
            pltpu.VMEM((1, W), F32),
        ),
        in_specs=[hbm] * 7 + [smem] + [hbm] * 6,
        out_specs=(vmem,) * 4,
        scratch_shapes=[
            pltpu.VMEM((X, ROWS, W), BF16),
            pltpu.VMEM((2, X, W, cols), BF16),
            pltpu.VMEM((X, COT_ROWS, W), BF16),
            pltpu.VMEM((X, ROWS, W), BF16),
            pltpu.VMEM((1, W), BF16),
            pltpu.VMEM((1, TMAX, TILE, TILE), BF16),
            pltpu.SMEM((1, TMAX), I32),
            pltpu.VMEM((SLOTS, 1, DOM), I32),
            pltpu.VMEM((SLOTS, 1, DOM), I32),
            pltpu.VMEM((SLOTS, 1, DOM), F32),
            pltpu.VMEM((1, DOM), I32),
            pltpu.SMEM((1, HUB), I32),
            pltpu.VMEM((ROWS, HUB * DOM), BF16),
            pltpu.VMEM((Z, ZROWS, W), BF16),
            pltpu.VMEM((Z, ZROWS, W), BF16),
            pltpu.VMEM((YC, B_ROWS, W), BF16),
            pltpu.VMEM((YC, B_ROWS, W), BF16),
            pltpu.VMEM((X, ROWS, W), BF16),
            pltpu.VMEM((X, ROWS, W), F32),
            pltpu.VMEM((YC, C_ROWS, W), BF16),
            pltpu.VMEM((YC, C_ROWS, W), BF16),
            pltpu.VMEM((Z, ZROWS, W), BF16),
            pltpu.VMEM((Z, ZROWS, W), BF16),
            pltpu.VMEM((ROWS, SLOTS * DOM), BF16),
            pltpu.VMEM((ROWS, ROWS + rest), BF16),
            pltpu.VMEM((ROWS + rest, ROWS), BF16),
            pltpu.VMEM((ROWS, W), F32),
            pltpu.VMEM((ROWS, cols), F32),
            pltpu.VMEM((Y, W, W), F32),
            pltpu.VMEM((Y, W, W), F32),
            pltpu.VMEM((Y, W, W), F32),
            pltpu.VMEM((Y, W, W), BF16),
            pltpu.VMEM((Y, W, W), BF16),
            pltpu.VMEM((W, W), F32),
            pltpu.VMEM((Z, 8, W), F32),
            pltpu.VMEM((W, W), F32),
            pltpu.SemaphoreType.DMA((13,)),
            pltpu.SemaphoreType.DMA((STAGES,)),
            pltpu.SemaphoreType.DMA((STAGES,)),
        ],
        compiler_params=pltpu.CompilerParams(
            collective_id=0, has_side_effects=True, vmem_limit_bytes=32 * 1024 * 1024
        ),
    )(
        *(
            array if array is tile_count else pltpu.with_memory_space_constraint(array, pltpu.HBM)
            for array in (
                features, w_self, w_neigh, bias.reshape(1, W), cotangent, tile_vals, tile_pos, tile_count,
                by_slot(send_rows), by_slot(recv_dest), by_slot(ghost_weight), recv_count, hub_rows, hub_weight,
            )
        )
    )
    output, grad_features, grad_self, grad_neigh, grad_bias = pl.pallas_call(
        save_kernel,
        out_shape=(
            jax.ShapeDtypeStruct((ROWS, W), BF16),
            jax.ShapeDtypeStruct((ROWS, W), BF16),
            jax.ShapeDtypeStruct((W, cols), F32),
            jax.ShapeDtypeStruct((W, cols), F32),
            jax.ShapeDtypeStruct((1, W), F32),
        ),
        in_specs=[vmem] * 4,
        out_specs=(hbm,) * 5,
        scratch_shapes=[
            pltpu.VMEM((W, cols), F32),
            pltpu.VMEM((W, cols), F32),
            pltpu.SemaphoreType.DMA((5,)),
        ],
    )(*(pltpu.with_memory_space_constraint(array, pltpu.VMEM) for array in results))
    return output, grad_features, grad_self, grad_neigh, grad_bias.reshape(W)


def solution(mesh):
    placed = (
        P("dom", "feat"),
        P("feat", None),
        P("feat", None),
        P("feat"),
        P("dom", "feat"),
        P("dom", None, None, None),
        P("dom", None),
        P("dom"),
        P("dom", None, None),
        P("dom", None, None),
        P("dom", None, None),
        P("dom", None),
        P("dom", None),
        P("dom", None),
    )
    return jax.shard_map(
        on_device,
        mesh=mesh,
        in_specs=placed,
        out_specs=(P("dom", "feat"), P("dom", "feat"), P("feat", None), P("feat", None), P("feat")),
        check_vma=False,
    )
```

time: 80 us -> 66 us (0.82)
  Pallas kernels: 75.9 us -> 64.6 us
  local copies, waits for them, and re-layouts: 2.59 us -> 0 us
    pallas_call x1, Pallas kernels: 73.9 us -> 63.7 us  [on_device(): pl.pallas_call(kernel, out_shape=(pltpu.VMEM((ROWS, W), BF16), pltpu.VMEM...]
    unnamed x8 -> x0, local copies, waits for them, and re-layouts: 2.59 us -> none
    pallas_call x1, Pallas kernels: 2.04 us -> 0.88 us  [on_device(): pl.pallas_call(save_kernel, out_shape=(jax.ShapeDtypeStruct((ROWS, W), BF...]
where the time goes in v3:
time: 66 us; the launch traced here: 65.9 us
  Pallas kernels  64.6 us (98%)
  between operations  1.29 us (2%)
    pallas_call x1, Pallas kernels, on_device(): pl.pallas_call(kernel, out_shape=(pltpu.VMEM((ROWS, W), BF16), pltpu.VMEM...  63.7 us

profile of v3, /device:TPU:1, one launch (start us, length us, event | category | flops | bytes accessed | tf_op | source)
XLA Modules:
  0.0 65.9 jit_solution(7019894098617678574)
XLA Ops:
  1.3 63.7 %shard_map.173 = (bf16[256,128]{1,0:T(8,128)(2,1)S(1)}, bf16[256,128]{1,0:T(8,128)(2,1)S(1)}, bf16[2,4,128,128]{3,2,1,0:T(8,128)(2,1)S(1)}, f32[1,128]{1,0:T(1,128)S(1)}) custom-call(bf16[256,128]{1,0:T(8,128)(2,1)} %feat_h.1, bf16[128,512]{1,0:T(8,128)(2,1)} %wself_h.1, bf16[128,512]{1,0:T(8,128)(2,1)} %wneigh_h.1, bf16[1,128]{1,0:T(2,128)(2,1)} %bitcast.8, ...), custom_call_target="tpu_custom_call" | custom-call | tf_op jit(solution)/shard_map/pallas_call | solution.py:365
  65.0 0.9 %shard_map.174 = (bf16[256,128]{1,0:T(8,128)(2,1)}, bf16[256,128]{1,0:T(8,128)(2,1)}, f32[128,512]{1,0:T(8,128)}, f32[128,512]{1,0:T(8,128)}, f32[1,128]{1,0:T(1,128)}) custom-call(bf16[256,128]{1,0:T(8,128)(2,1)S(1)} %get-tuple-element.14.out_v, bf16[256,128]{1,0:T(8,128)(2,1)S(1)} %get-tuple-element.15.gf_v, ...), custom_call_target="tpu_custom_call" | custom-call | tf_op jit(solution)/shard_map/pallas_call | solution.py:428

commit v4 on v3

--- a/solution.py
+++ b/solution.py
@@ -18,8 +18,11 @@
 B_ROWS = SLOTS * Z + HUB * Z
 C_ROWS = B_ROWS + 16
 COT_ROWS = ROWS + 16
-
-(ST_A, ST_B, ST_XF, ST_XW, ST_XC, ST_CW, ST_P, ST_C, ST_D, ST_RC, ST_RY, ST_RZ, ST_GZ, ST_GC, ST_GY) = range(15)
+WROWS = W // Y
+OWNERS = 8
+GROWS = W // OWNERS
+
+(ST_A, ST_B, ST_XF, ST_XW, ST_XC, ST_CW, ST_P, ST_C, ST_D, ST_RC, ST_RY, ST_RZ, ST_GZ, ST_GC, ST_YW, ST_GY) = range(16)
 STAGES = ST_GY + Y
 
 
@@ -64,7 +67,7 @@
     out_v, gf_v, wtot, gb_v,
     feat_x, w_x, cot_x, neigh_x, bias_v, tiles, pos_s, send_v, dest_v, gw_v, rc_v, hub_s, hw,
     send_a, recv_a, send_b, recv_b, gp, own_pre, send_c, recv_c, send_d, recv_d,
-    g_m, m_m, mt_m, base, pself, wsend, wown, rcore, send_ry, ry, ysum, rz, gz,
+    g_m, m_m, mt_m, base, pself, wsend, wown, rcore, send_ry, ry, ysum, rz,
     in_sem, send_sem, recv_sem,
 ):
     d = lax.axis_index("dom")
@@ -155,12 +158,13 @@
     pending.append((ST_A, send_a.at[pl.ds(0, Z - 1)]))
     recv_a[pl.ds(z, 1)] = send_a[pl.ds(z, 1)]
 
+    quarter = pl.ds(pl.multiple_of(y * WROWS, WROWS), WROWS)
+    for copy in load_w:
+        copy.wait()
+    around(X, lambda k: push(ST_XW, w_x.at[c, f, quarter], w_x.at[c, f, quarter], d, x_peer(k)))
+    pending.append((ST_XW, w_x.at[0, 0, pl.ds(0, (X - 1) * WROWS)]))
     around(X, lambda k: push(ST_XF, feat_x.at[f], feat_x.at[f], d, x_peer(k)))
     pending.append((ST_XF, feat_x.at[pl.ds(0, X - 1)]))
-    for copy in load_w:
-        copy.wait()
-    around(X, lambda k: push(ST_XW, w_x.at[c, f], w_x.at[c, f], d, x_peer(k)))
-    pending.append((ST_XW, w_x.at[0, pl.ds(0, X - 1)]))
     for copy in load_cot:
         copy.wait()
     bias_rows = jnp.concatenate([bias_v[...].astype(F32), jnp.zeros((15, W), F32)], axis=0)
@@ -181,6 +185,15 @@
             row_of == dest_row, packed[SLOTS + s : SLOTS + s + 1], 0.0
         ).astype(BF16)
 
+    arrived(ST_XW, w_x.at[0, 0, pl.ds(0, (X - 1) * WROWS)])
+
+    def weight_on(j):
+        shard = w_x.at[c, x_peer(j), quarter]
+        around(Y, lambda k: push(ST_YW, shard, shard, y_peer(k), f))
+
+    around(X, weight_on)
+    pending.append((ST_YW, w_x.at[0, pl.ds(0, X - 1), pl.ds(0, (Y - 1) * WROWS)]))
+
     arrived(ST_A, recv_a.at[pl.ds(0, Z - 1)])
     got = recv_a[...].astype(F32)
     for s in range(SLOTS):
@@ -213,7 +226,7 @@
     around(X, lambda k: push(ST_P, neigh_x.at[f], neigh_x.at[f], d, x_peer(k)))
     pending.append((ST_P, neigh_x.at[pl.ds(0, X - 1)]))
 
-    arrived(ST_XW, w_x.at[0, pl.ds(0, X - 1)])
+    arrived(ST_YW, w_x.at[0, pl.ds(0, X - 1), pl.ds(0, (Y - 1) * WROWS)])
     around(X, lambda k: push(ST_CW, w_x.at[c, x_peer(k)], w_x.at[c, x_peer(k)], partner, f))
     pending.append((ST_CW, w_x.at[0, pl.ds(0, X - 1)]))
     mt_m[...] = m_m[...].T
@@ -244,6 +257,12 @@
     for j in range(X):
         wown[j] = tdot(rows_own, gp[j])
 
+    arrived(ST_RC, rcore)
+    send_ry[...] = (rcore[...] + wown[...]).astype(BF16)
+    around(Y, lambda k: push(ST_RY, send_ry.at[lax.rem(y + k, Y)], ry.at[y], y_peer(k), f))
+    pending.append((ST_RY, ry.at[pl.ds(0, Y - 1)]))
+    ry[pl.ds(y, 1)] = send_ry[pl.ds(y, 1)]
+
     gp_full = jnp.concatenate([gp[j] for j in range(X)], axis=1)
     neigh_grad = dot_t(gp_full, w_x[1, f]).astype(BF16)
     back = dot(mt_m[...], neigh_grad)
@@ -264,24 +283,20 @@
     pending.append((ST_C, send_c.at[pl.ds(0, YC - 1)]))
     recv_c[pl.ds(yc, 1)] = send_c[pl.ds(yc, 1)]
 
-    arrived(ST_RC, rcore)
-    send_ry[...] = (rcore[...] + wown[...]).astype(BF16)
-    around(Y, lambda k: push(ST_RY, send_ry.at[lax.rem(y + k, Y)], ry.at[y], y_peer(k), f))
-    pending.append((ST_RY, ry.at[pl.ds(0, Y - 1)]))
-    ry[pl.ds(y, 1)] = send_ry[pl.ds(y, 1)]
     base[...] = back[:ROWS] + dot_t(gp_full, w_x[0, f])
 
     arrived(ST_RY, ry.at[pl.ds(0, Y - 1)])
-    ysum[...] = jnp.sum(ry[...].astype(F32), axis=0)
-    around(
-        Z,
-        lambda k: push(
-            ST_RZ, ysum.at[pl.ds(pl.multiple_of(lax.rem(z + k, Z) * 8, 8), 8)], rz.at[z], z_peer(k), f
-        ),
-    )
+    ysum[...] = jnp.sum(ry[...].astype(F32), axis=0).astype(BF16)
+
+    def chunk(owner):
+        return pl.ds(pl.multiple_of(lax.rem(owner, OWNERS) * GROWS, GROWS), GROWS)
+
+    around(Z, lambda k: push(ST_RZ, ysum.at[chunk(z + k)], rz.at[z], z_peer(k), f))
     pending.append((ST_RZ, rz.at[pl.ds(0, Z - 1)]))
-    mine = pl.ds(pl.multiple_of(z * 8, 8), 8)
+    mine = chunk(z)
     rz[pl.ds(z, 1)] = ysum[mine][None]
+    preact = own_pre[f]
+    out_v[...] = (preact * jax.nn.sigmoid(preact)).astype(BF16)
 
     arrived(ST_C, recv_c.at[pl.ds(0, YC - 1)])
     groups = []
@@ -293,17 +308,30 @@
     bias_sum = bias_sum[0:1] + bias_sum[1:2]
     groups.append(tdot(pick, hub_sum.astype(BF16)).reshape(Z, 8, W) + two_rows(bias_sum, HUB)[None])
     send_d[...] = jnp.concatenate(groups, axis=1).astype(BF16)
+
+    arrived(ST_RZ, rz.at[pl.ds(0, Z - 1)])
+    scale = 1.0 / math.sqrt(DOM * ROWS)
+    wtot[c, y, mine] = (jnp.sum(rz[...].astype(F32), axis=0) * scale).astype(BF16)
+
+    def near(k):
+        return z_peer(jnp.where(k > OWNERS // 2, k + Z - OWNERS, k))
+
+    around(OWNERS, lambda k: push(ST_GZ, wtot.at[c, y, mine], wtot.at[c, y, mine], near(k), f))
+    pending.append((ST_GZ, rz.at[pl.ds(0, OWNERS - 1)]))
     around(Z, lambda k: push(ST_D, send_d.at[lax.rem(z + k, Z)], recv_d.at[z], z_peer(k), f))
     pending.append((ST_D, send_d.at[pl.ds(0, Z - 1)]))
     recv_d[pl.ds(z, 1)] = send_d[pl.ds(z, 1)]
-    preact = own_pre[f]
-    out_v[...] = (preact * jax.nn.sigmoid(preact)).astype(BF16)
-
-    arrived(ST_RZ, rz.at[pl.ds(0, Z - 1)])
-    scale = 1.0 / math.sqrt(DOM * ROWS)
-    gz[mine] = jnp.sum(rz[...], axis=0) * scale
-    around(Z, lambda k: push(ST_GZ, gz.at[mine], gz.at[mine], z_peer(k), f))
-    pending.append((ST_GZ, rz.at[pl.ds(0, Z - 1)]))
+
+    arrived(ST_GZ, rz.at[pl.ds(0, OWNERS - 1)])
+    for k in (2, 1, 3):
+        push(ST_GY + k, wtot.at[c, y], wtot.at[c, y], y_peer(k), f)
+        pending.append((ST_GY + k, wtot.at[0, 0]))
+    push(ST_GC, wtot.at[c, y], wtot.at[c, y], partner, f)
+    for k in (1, 3, 2):
+        source = lax.rem(y + Y - k, Y)
+        arrived(ST_GY + k, wtot.at[c, source])
+        push(ST_GC, wtot.at[c, source], wtot.at[c, source], partner, f)
+    pending.append((ST_GC, wtot.at[0]))
 
     arrived(ST_D, recv_d.at[pl.ds(0, Z - 1)])
     got = recv_d[...].astype(F32)
@@ -316,17 +344,6 @@
     gf_v[...] = total.astype(BF16)
     gb_v[...] = (last[HUB : HUB + 1] + last[HUB + 1 : HUB + 2]) * scale
 
-    arrived(ST_GZ, gz.at[pl.ds(0, (Z - 1) * 8)])
-    wtot[c, y] = gz[...].astype(BF16)
-    for k in (2, 1, 3):
-        push(ST_GY + k, wtot.at[c, y], wtot.at[c, y], y_peer(k), f)
-        pending.append((ST_GY + k, wtot.at[0, 0]))
-    push(ST_GC, wtot.at[c, y], wtot.at[c, y], partner, f)
-    for k in (1, 3, 2):
-        source = lax.rem(y + Y - k, Y)
-        arrived(ST_GY + k, wtot.at[c, source])
-        push(ST_GC, wtot.at[c, source], wtot.at[c, source], partner, f)
-    pending.append((ST_GC, wtot.at[0]))
     arrived(ST_GC, wtot.at[1 - c])
     for stage, ref in pending:
         sent(stage, ref)
@@ -406,9 +423,8 @@
             pltpu.VMEM((Y, W, W), F32),
             pltpu.VMEM((Y, W, W), BF16),
             pltpu.VMEM((Y, W, W), BF16),
-            pltpu.VMEM((W, W), F32),
-            pltpu.VMEM((Z, 8, W), F32),
-            pltpu.VMEM((W, W), F32),
+            pltpu.VMEM((W, W), BF16),
+            pltpu.VMEM((Z, GROWS, W), BF16),
             pltpu.SemaphoreType.DMA((13,)),
             pltpu.SemaphoreType.DMA((STAGES,)),
             pltpu.SemaphoreType.DMA((STAGES,)),

time: 66 us -> 62.1 us (0.941)
  Pallas kernels: 64.6 us -> 60.7 us
    pallas_call x1, Pallas kernels: 63.7 us -> 59.8 us  [on_device(): pl.pallas_call(kernel, out_shape=(pltpu.VMEM((ROWS, W), BF16), pltpu.VMEM...]
where the time goes in v4:
time: 62.1 us; the launch traced here: 62 us
  Pallas kernels  60.7 us (98%)
  between operations  1.29 us (2%)
    pallas_call x1, Pallas kernels, on_device(): pl.pallas_call(kernel, out_shape=(pltpu.VMEM((ROWS, W), BF16), pltpu.VMEM...  59.8 us

profile of v4, /device:TPU:1, one launch (start us, length us, event | category | flops | bytes accessed | tf_op | source)
XLA Modules:
  0.0 62.0 jit_solution(6740311836986334106)
XLA Ops:
  1.3 59.8 %shard_map.173 = (bf16[256,128]{1,0:T(8,128)(2,1)S(1)}, bf16[256,128]{1,0:T(8,128)(2,1)S(1)}, bf16[2,4,128,128]{3,2,1,0:T(8,128)(2,1)S(1)}, f32[1,128]{1,0:T(1,128)S(1)}) custom-call(bf16[256,128]{1,0:T(8,128)(2,1)} %feat_h.1, bf16[128,512]{1,0:T(8,128)(2,1)} %wself_h.1, bf16[128,512]{1,0:T(8,128)(2,1)} %wneigh_h.1, bf16[1,128]{1,0:T(2,128)(2,1)} %bitcast.8, ...), custom_call_target="tpu_custom_call" | custom-call | tf_op jit(solution)/shard_map/pallas_call | solution.py:382
  61.1 0.9 %shard_map.174 = (bf16[256,128]{1,0:T(8,128)(2,1)}, bf16[256,128]{1,0:T(8,128)(2,1)}, f32[128,512]{1,0:T(8,128)}, f32[128,512]{1,0:T(8,128)}, f32[1,128]{1,0:T(1,128)}) custom-call(bf16[256,128]{1,0:T(8,128)(2,1)S(1)} %get-tuple-element.14.out_v, bf16[256,128]{1,0:T(8,128)(2,1)S(1)} %get-tuple-element.15.gf_v, ...), custom_call_target="tpu_custom_call" | custom-call | tf_op jit(solution)/shard_map/pallas_call | solution.py:444
